TPU v7x, 256 devices: a whole 4x4x8 slice. The times are simulated.
256 devices in a mesh: rep: 16 (over x, y_lo, core), fsdp: 16 (over y_hi, z).
Axes of the slice: x: 4, y: 4 (y_hi: 2, y_lo: 2; y = y_hi * 2 + y_lo), z: 8, core: 2. Of those that a mesh axis runs over, the one named last changes fastest.
Arguments:
- local_params: bfloat16 [16, 256, 28672], P('rep', 'fsdp'), may hold values from -6 to 6
- base_params: float32 [256, 28672], P('fsdp'), may hold values from -6 to 6
- error_buffer: float32 [16, 256, 28672], P('rep', 'fsdp'), may hold values from -4 to 4
- momentum: float32 [256, 28672], P('fsdp'), may hold values from -3 to 3
Outputs:
- new_base: float32 [256, 28672], P('fsdp')
- new_error: float32 [16, 256, 28672], P('rep', 'fsdp')
- new_momentum: float32 [256, 28672], P('fsdp')
All inputs are finite; a program needn't handle non-finite values.
Results may differ from a plain program's by a relative error of at most 0.0003.
Values sent between devices are 32-bit elements; how exact they have to be, the bound alone decides.
No kernel may reach another device: no remote copies, remote signals or barrier semaphores. Data moves between devices by JAX's collectives and lax.ppermute only.
A program may use at most 64 MiB of HBM per device.

v0:
```python
import math

import jax
import jax.numpy as jnp
from jax import lax
from jax.sharding import PartitionSpec as P

TILE = 64
BAND = 16


outer_rate = 0.7
outer_beta = 0.9


def band_table():
    freq = lax.broadcasted_iota(jnp.float32, (BAND, TILE), 0)
    sample = lax.broadcasted_iota(jnp.float32, (BAND, TILE), 1)
    scale = jnp.where(freq == 0, math.sqrt(1.0 / TILE), math.sqrt(2.0 / TILE))
    return scale * jnp.cos(math.pi * (2.0 * sample + 1.0) * freq / (2.0 * TILE))


def forward_band(field, lowband):
    row_count, col_count = field.shape
    tiles = field.reshape(row_count // TILE, TILE, col_count // TILE, TILE)
    coeffs = jnp.einsum(
        "ka,iajb,lb->ikjl", lowband, tiles, lowband, precision=lax.Precision.HIGHEST
    )
    return coeffs.reshape(row_count // TILE, BAND, col_count // TILE * BAND)


def inverse_band(coeffs, lowband, row_count, col_count):
    blocks = coeffs.reshape(row_count // TILE, BAND, col_count // TILE, BAND)
    tiles = jnp.einsum(
        "ka,ikjl,lb->iajb", lowband, blocks, lowband, precision=lax.Precision.HIGHEST
    )
    return tiles.reshape(row_count, col_count)


def local(local_params, base_params, error_buffer, momentum):
    lowband = band_table()
    pseudo_grad = base_params - local_params[0].astype(jnp.float32) + error_buffer[0]
    replicas = lax.axis_size("rep")
    columns = lax.all_to_all(pseudo_grad, "fsdp", split_axis=1, concat_axis=0, tiled=True)
    full_rows, narrow_cols = columns.shape
    coefficients = forward_band(columns, lowband)
    summed = lax.psum(coefficients, "rep")
    error_cols = columns - inverse_band(coefficients, lowband, full_rows, narrow_cols)
    outer_cols = inverse_band(summed / replicas, lowband, full_rows, narrow_cols)
    new_error, outer_grad = (
        lax.all_to_all(error_cols, "fsdp", split_axis=0, concat_axis=1, tiled=True),
        lax.all_to_all(outer_cols, "fsdp", split_axis=0, concat_axis=1, tiled=True),
    )
    new_momentum = outer_beta * momentum + outer_grad
    new_base = base_params - outer_rate * (outer_grad + outer_beta * new_momentum)
    return (new_base, new_error[None], new_momentum)


def solution(mesh):
    in_specs = (P("rep", "fsdp", None), P("fsdp", None), P("rep", "fsdp", None), P("fsdp", None))
    out_specs = (P("fsdp", None), P("rep", "fsdp", None), P("fsdp", None))
    return jax.shard_map(local, mesh=mesh, in_specs=in_specs, out_specs=out_specs, check_vma=False)
```

profile of v0, /device:TPU:1, one launch (start us, length us, event | category | flops | bytes accessed | tf_op | source)
XLA Modules:
  0.0 315.1 jit_solution(11446580422293092555)
XLA Ops:
  7.2 2.5 fusion.2
  9.7 1.4 copy.39
  11.1 11.7 %all-to-all-start = ((f32[16,16,1792]{2,0,1:T(8,128)}), f32[16,16,1792]{2,0,1:T(8,128)S(1)}, u32[]{:S(2)}, u32[]{:S(2)}) async-start(f32[16,16,1792]{2,0,1:T(8,128)} %bitcast.43), calls=%async_computation | async-start | bytes 3670016 | tf_op jit(solution)/shard_map/all_to_all | solution.py:44
  22.9 43.2 %all-to-all-done = f32[16,16,1792]{2,0,1:T(8,128)S(1)} async-done(((f32[16,16,1792]{2,0,1:T(8,128)}), f32[16,16,1792]{2,0,1:T(8,128)S(1)}, u32[]{:S(2)}, u32[]{:S(2)}) %all-to-all-start) | async-done | bytes 1835040 | tf_op jit(solution)/shard_map/all_to_all | solution.py:44
  66.1 2.9 reshape.34
  69.0 6.3 %fusion = f32[4,28,64,16]{2,3,1,0:T(8,128)S(1)} fusion(f32[4,64,28,64]{3,2,1,0:T(8,128)} %reshape.34, f32[16]{0:T(128)S(1)} %get-tuple-element.6, f32[64]{0:T(128)S(1)} %multiply_add_fusion.1, f32[16]{0:T(128)S(1)} %get-tuple-element.5), kind=kOutput, calls=%fused_computation | convolution fusion | flops 88083456 | bytes 2294144 | tf_op jit(solution)/shard_map/ka,iajb,lb->ikjl/dot_general | solution.py:26
  75.3 4.2 %convolution_bitcast_fusion.2 = f32[4,16,28,16]{2,3,1,0:T(8,128)S(1)} fusion(f32[4,28,64,16]{2,3,1,0:T(8,128)S(1)} %fusion, f32[16]{0:T(128)S(1)} %get-tuple-element.6, f32[64]{0:T(128)S(1)} %multiply_add_fusion.1, f32[16]{0:T(128)S(1)} %get-tuple-element.5), kind=kOutput, calls=%fused_computation.9 | convolution fusion | flops 22023168 | bytes 573824 | tf_op jit(solution)/shard_map/ka,iajb,lb->ikjl/dot_general | solution.py:26
  79.6 0.6 copy.27
  80.2 1.0 fusion.5
  81.2 5.9 %convolution_bitcast_fusion = f32[4,64,28,64]{3,1,2,0:T(8,128)S(1)} fusion(f32[4,28,16,64]{3,2,1,0:T(8,128)S(1)} %fusion.5, f32[16]{0:T(128)S(1)} %get-tuple-element.6, f32[64]{0:T(128)S(1)} %multiply_add_fusion.1, f32[16]{0:T(128)S(1)} %get-tuple-element.5), kind=kOutput, calls=%fused_computation.2 | convolution fusion | flops 88083456 | bytes 2294144 | tf_op jit(solution)/shard_map/ka,ikjl,lb->iajb/dot_general | solution.py:34
  87.1 4.1 %copy.28 = f32[4,64,28,64]{3,2,1,0:T(8,128)} copy(f32[4,64,28,64]{3,1,2,0:T(8,128)S(1)} %convolution_bitcast_fusion) | data formatting | bytes 3670016 | tf_op jit(solution)/shard_map/ka,ikjl,lb->iajb/transpose | solution.py:34
  91.2 4.6 %reshape.37 = f32[16,16,1792]{2,1,0:T(8,128)} reshape(f32[4,64,28,64]{3,2,1,0:T(8,128)} %copy.28) | data formatting | bytes 3670016 | tf_op jit(solution)/shard_map/reshape | solution.py:37
  95.8 2.9 bitcast_subtract_fusion
  98.8 7.2 %all-to-all-start.2 = ((f32[16,16,1792]{2,1,0:T(8,128)}), f32[16,16,1792]{2,1,0:T(8,128)S(1)}, u32[]{:S(2)}, u32[]{:S(2)}) async-start(f32[16,16,1792]{2,1,0:T(8,128)} %bitcast_subtract_fusion), calls=%async_computation.2 | async-start | bytes 3670016 | tf_op jit(solution)/shard_map/all_to_all | solution.py:51
  106.0 0.0 all-reduce.2.cloned.1.call-start
  106.1 0.5 copy.23
  106.5 1.2 reshape.35
  107.8 126.1 %all-reduce.2.cloned.1.call-done = f32[4,16,448]{2,1,0:T(8,128)} async-done(((f32[4,16,448]{2,1,0:T(8,128)}), f32[4,16,448]{2,1,0:T(8,128)}) %all-reduce.2.cloned.1.call-update) | async-done | bytes 114704 | tf_op jit(solution)/shard_map/psum | solution.py:47
  233.9 0.9 broadcast_multiply_fusion
  234.8 0.3 copy.31
  235.1 1.0 fusion.8
  236.1 5.9 %convolution_bitcast_fusion.1 = f32[4,64,28,64]{3,1,2,0:T(8,128)S(1)} fusion(f32[4,28,16,64]{3,2,1,0:T(8,128)S(1)} %fusion.8, f32[16]{0:T(128)S(1)} %get-tuple-element.6, f32[64]{0:T(128)S(1)} %multiply_add_fusion.1, f32[16]{0:T(128)S(1)} %get-tuple-element.5), kind=kOutput, calls=%fused_computation.3 | convolution fusion | flops 88083456 | bytes 2294144 | tf_op jit(solution)/shard_map/ka,ikjl,lb->iajb/dot_general | solution.py:34
  242.1 4.1 %copy.25 = f32[4,64,28,64]{3,2,1,0:T(8,128)} copy(f32[4,64,28,64]{3,1,2,0:T(8,128)S(1)} %convolution_bitcast_fusion.1) | data formatting | bytes 3670016 | tf_op jit(solution)/shard_map/ka,ikjl,lb->iajb/transpose | solution.py:34
  246.2 4.6 %all_to_all.39 = f32[16,16,1792]{2,1,0:T(8,128)} reshape(f32[4,64,28,64]{3,2,1,0:T(8,128)} %copy.25) | data formatting | bytes 3670016 | tf_op jit(solution)/shard_map/all_to_all | solution.py:52
  250.8 9.0 %all-to-all-start.1 = ((f32[16,16,1792]{2,1,0:T(8,128)}), f32[16,16,1792]{2,1,0:T(8,128)}, u32[]{:S(2)}, u32[]{:S(2)}) async-start(f32[16,16,1792]{2,1,0:T(8,128)} %all_to_all.39), calls=%async_computation.1 | async-start | bytes 3670016 | tf_op jit(solution)/shard_map/all_to_all | solution.py:52
  259.9 2.3 copy.29
  262.1 3.1 broadcast_in_dim.13
  265.2 38.2 %all-to-all-done.1 = f32[16,16,1792]{2,1,0:T(8,128)} async-done(((f32[16,16,1792]{2,1,0:T(8,128)}), f32[16,16,1792]{2,1,0:T(8,128)}, u32[]{:S(2)}, u32[]{:S(2)}) %all-to-all-start.1) | async-done | bytes 1835040 | tf_op jit(solution)/shard_map/all_to_all | solution.py:52
  303.4 1.8 copy.33
  305.2 0.3 copy-done
  305.5 0.6 copy-done.1
  306.0 2.3 multiply_subtract_fusion
  (6 shorter events, 0.0 us)
Async XLA Ops:
  11.1 55.0 %all-to-all-start = ((f32[16,16,1792]{2,0,1:T(8,128)}), f32[16,16,1792]{2,0,1:T(8,128)S(1)}, u32[]{:S(2)}, u32[]{:S(2)}) async-start(f32[16,16,1792]{2,0,1:T(8,128)} %bitcast.43), calls=%async_computation | async-start | bytes 3670016 | tf_op jit(solution)/shard_map/all_to_all | solution.py:44
  98.8 152.0 %all-to-all-start.2 = ((f32[16,16,1792]{2,1,0:T(8,128)}), f32[16,16,1792]{2,1,0:T(8,128)S(1)}, u32[]{:S(2)}, u32[]{:S(2)}) async-start(f32[16,16,1792]{2,1,0:T(8,128)} %bitcast_subtract_fusion), calls=%async_computation.2 | async-start | bytes 3670016 | tf_op jit(solution)/shard_map/all_to_all | solution.py:51
  106.0 127.9 %all-reduce.2.cloned.1.call-start = ((), (), s32[]{:S(2)}) async-start(), calls=%async_computation.3 | async-start | bytes 262144 | tf_op jit(solution)/shard_map/psum | solution.py:47
  250.8 52.6 %all-to-all-start.1 = ((f32[16,16,1792]{2,1,0:T(8,128)}), f32[16,16,1792]{2,1,0:T(8,128)}, u32[]{:S(2)}, u32[]{:S(2)}) async-start(f32[16,16,1792]{2,1,0:T(8,128)} %all_to_all.39), calls=%async_computation.1 | async-start | bytes 3670016 | tf_op jit(solution)/shard_map/all_to_all | solution.py:52
  303.4 2.1 copy-start
  303.4 2.6 copy-start.1
Sparse Core Ops, SparseCore 0:
  110.0 123.8 all-reduce.1
where the time goes:
time: 316 us; the launch traced here: 315 us
  waiting for transfers between devices  208 us (66%)
  local copies, waits for them, and re-layouts  32.3 us (10%)
  starting transfers between devices  28.1 us (9%)
  matrix products  24.4 us (8%)
  between operations  14.1 us (4%)
  other arithmetic  8.63 us (3%)
    psum x1, waiting for transfers between devices, local(): summed = lax.psum(coefficients, 'rep')  126 us
    all_to_all x1, waiting for transfers between devices, local(): lax.all_to_all(pseudo_grad, 'fsdp', split_axis=1, concat_axis=0, tiled=True)  43.2 us
    all_to_all x1, waiting for transfers between devices, local(): lax.all_to_all(outer_cols, 'fsdp', split_axis=0, concat_axis=1, tiled=True)  38.2 us
    dot_general x4, matrix products, inverse_band(): jnp.einsum('ka,ikjl,lb->iajb', lowband, blocks, lowband, precision=lax.Pr...  13.8 us
    all_to_all x1, starting transfers between devices, local(): lax.all_to_all(pseudo_grad, 'fsdp', split_axis=1, concat_axis=0, tiled=True)  11.7 us
    dot_general x2, matrix products, forward_band(): jnp.einsum('ka,iajb,lb->ikjl', lowband, tiles, lowband, precision=lax.Pre...  10.6 us
    all_to_all x1, starting transfers between devices, local(): lax.all_to_all(outer_cols, 'fsdp', split_axis=0, concat_axis=1, tiled=True)  9.04 us
    transpose x2, local copies, waits for them, and re-layouts, inverse_band(): jnp.einsum('ka,ikjl,lb->iajb', lowband, blocks, lowband, precision=lax.Pr...  8.18 us
  transfers between devices with their start and end apart: 4, of which 3 were waited for; matrix products, arithmetic and copies ran while one was open for 6% of the time, Pallas kernels for 0%

commit v1 on v0

v1 whole, which is shorter than its diff:
```python
import functools
import math

import jax
import jax.numpy as jnp
import ml_dtypes
import numpy as np
from jax import lax
from jax.experimental import pallas as pl
from jax.experimental.pallas import tpu as pltpu
from jax.sharding import PartitionSpec as P

TILE = 64
BAND = 16
OUTER_RATE = 0.7
OUTER_BETA = 0.9

PARTS = 4
ROWS = TILE // PARTS
GROUP_TILES = 8
GROUP = GROUP_TILES * TILE
WIDE = GROUP_TILES * BAND
VMEM_LIMIT = 40 * 1024 * 1024

HBM = pl.BlockSpec(memory_space=pltpu.HBM)
VMEM = pl.BlockSpec(memory_space=pltpu.VMEM)


def split_np(table):
    high = table.astype(np.float32).astype(ml_dtypes.bfloat16)
    low = (table - high.astype(np.float64)).astype(np.float32).astype(ml_dtypes.bfloat16)
    return high, low


def tables():
    freq = np.arange(BAND, dtype=np.float64)[:, None]
    sample = np.arange(TILE, dtype=np.float64)[None, :]
    scale = np.where(freq == 0, math.sqrt(1.0 / TILE), math.sqrt(2.0 / TILE))
    lowband = scale * np.cos(math.pi * (2.0 * sample + 1.0) * freq / (2.0 * TILE))
    high, low = split_np(np.kron(np.eye(GROUP_TILES), lowband.T))
    col_fwd = np.concatenate([high, low], axis=1)
    col_inv = np.stack([np.concatenate([t.T, t.T], axis=0) for t in (high, low)])
    blocks = [lowband[:, ROWS * part : ROWS * (part + 1)] for part in range(PARTS)]
    rows_fwd = np.stack(blocks).astype(np.float32)
    rows_inv = np.stack([b.T for b in blocks]).astype(np.float32)
    return col_fwd, col_inv, rows_fwd, rows_inv


def split(value):
    high = value.astype(jnp.bfloat16)
    low = (value - high.astype(jnp.float32)).astype(jnp.bfloat16)
    return high, low


def dot(a, b):
    return jnp.dot(a, b, preferred_element_type=jnp.float32)


def apply_rows(table, value):
    deep = value.reshape(-1, table.shape[1], value.shape[1])
    total = None
    for a in range(table.shape[1]):
        term = table[None, :, a : a + 1] * deep[:, a : a + 1, :]
        total = term if total is None else total + term
    return total.reshape(-1, value.shape[1])


def position():
    part = lax.axis_index("fsdp") % PARTS
    core = lax.axis_index("rep") % 2
    return part, core


def quarter_cols(part, s, width):
    size = width // PARTS
    return pl.ds(pl.multiple_of((part ^ s) * size, GROUP), size)


def forward_kernel(base, local, err, col, rows, out, base_v, local_v, err_v, sems):
    part, core = position()
    width = base.shape[1]
    copies = []
    for s in range(PARTS):
        cols = quarter_cols(part, s, width)
        copies.append(
            [
                pltpu.make_async_copy(base.at[:, cols], base_v.at[s], sems.at[s, 0]),
                pltpu.make_async_copy(err.at[0, :, cols], err_v.at[s], sems.at[s, 1]),
                pltpu.make_async_copy(local.at[0, :, cols], local_v.at[s], sems.at[s, 2]),
            ]
        )
    for step in copies:
        for copy in step:
            copy.start()
    table = rows[part]
    for s in range(PARTS):
        for copy in copies[s]:
            copy.wait()
        field = base_v[s] - local_v[s].astype(jnp.float32) + err_v[s]
        groups = field.shape[1] // GROUP
        stacked = jnp.concatenate([field[:, GROUP * g : GROUP * (g + 1)] for g in range(groups)], axis=0)
        count = stacked.shape[0]
        both = dot(jnp.concatenate(split(stacked), axis=0), col[...])
        both = both[:, :WIDE] + both[:, WIDE:]
        coeffs = apply_rows(table, both[:count] + both[count:])
        half = count // 2
        out[s, core] = coeffs[:half]
        out[s, 1 - core] = coeffs[half:]


def inverse_rows(table, col, coeffs):
    both = jnp.concatenate(split(apply_rows(table, coeffs)), axis=1)
    return dot(both, col[0]) + dot(both, col[1])


def error_kernel(k0, k1, k2, k3, base, local, err, col, rows, out, base_v, local_v, err_v, out_v, sems):
    part, core = position()
    width = base.shape[1]
    copies, writes = [], []
    for s in range(PARTS):
        cols = quarter_cols(part, s, width)
        copies.append(
            [
                pltpu.make_async_copy(base.at[:, cols], base_v.at[s], sems.at[s, 0]),
                pltpu.make_async_copy(err.at[0, :, cols], err_v.at[s], sems.at[s, 1]),
                pltpu.make_async_copy(local.at[0, :, cols], local_v.at[s], sems.at[s, 2]),
            ]
        )
        writes.append(pltpu.make_async_copy(out_v.at[s], out.at[0, :, cols], sems.at[s, 3]))
    for step in copies:
        for copy in step:
            copy.start()
    table = rows[part]
    for s, k in enumerate((k0, k1, k2, k3)):
        coeffs = jnp.concatenate([k[core], k[1 - core]], axis=0)
        kept = inverse_rows(table, col, coeffs)
        for copy in copies[s]:
            copy.wait()
        for g in range(coeffs.shape[0] // ROWS):
            at = slice(GROUP * g, GROUP * (g + 1))
            field = base_v[s, :, at] - local_v[s, :, at].astype(jnp.float32) + err_v[s, :, at]
            out_v[s, :, at] = field - kept[ROWS * g : ROWS * (g + 1)]
        writes[s].start()
    for write in writes:
        write.wait()


def update_kernel(replicas, own, other, base, mom, col, rows, base_out, mom_out, base_w, mom_w, sems):
    part, core = position()
    width = base.shape[1]
    table = rows[part]
    writes = []
    for s in range(PARTS):
        cols = quarter_cols(part, s, width)
        both = jnp.stack([own[s], other[s]]) * (1.0 / replicas)
        first = jnp.where(core == 0, both[0], both[1])
        second = jnp.where(core == 0, both[1], both[0])
        outer = inverse_rows(table, col, jnp.concatenate([first, second], axis=0))
        size = width // PARTS
        for g in range(size // GROUP):
            at = slice(GROUP * g, GROUP * (g + 1))
            src = pl.ds(pl.multiple_of((part ^ s) * size + GROUP * g, GROUP), GROUP)
            grad = outer[ROWS * g : ROWS * (g + 1)]
            new_momentum = OUTER_BETA * mom[:, src] + grad
            mom_w[s, :, at] = new_momentum
            base_w[s, :, at] = base[:, src] - OUTER_RATE * (grad + OUTER_BETA * new_momentum)
        for i, (src, dst) in enumerate(((base_w, base_out), (mom_w, mom_out))):
            writes.append(pltpu.make_async_copy(src.at[s], dst.at[:, cols], sems.at[s, i]))
            writes[-1].start()
    for write in writes:
        write.wait()


def call(kernel, name, inputs, in_specs, out_specs, out_shape, scratch, flops, moved):
    return pl.pallas_call(
        kernel,
        in_specs=in_specs,
        out_specs=out_specs,
        out_shape=out_shape,
        scratch_shapes=scratch,
        compiler_params=pltpu.CompilerParams(vmem_limit_bytes=VMEM_LIMIT),
        cost_estimate=pl.CostEstimate(flops=flops, bytes_accessed=moved, transcendentals=0),
        name=name,
    )(*inputs)


def in_hbm(value):
    return pltpu.with_memory_space_constraint(value, pltpu.HBM)


def local(local_params, base_params, error_buffer, momentum):
    rows, width = base_params.shape
    replicas = lax.axis_size("rep")
    shards = lax.axis_size("fsdp")
    quarter_rows = width // PARTS // GROUP * ROWS
    col_fwd, col_inv, rows_fwd, rows_inv = (jnp.asarray(t) for t in tables())
    f32 = lambda *shape: jax.ShapeDtypeStruct(shape, jnp.float32)
    buffer = lambda dtype=jnp.float32: pltpu.VMEM((PARTS, rows, width // PARTS), dtype)
    cells = rows * width

    partial = call(
        forward_kernel, "forward",
        (in_hbm(base_params), in_hbm(local_params), in_hbm(error_buffer), col_fwd, rows_fwd),
        [HBM, HBM, HBM, VMEM, VMEM],
        VMEM, pltpu.VMEM((PARTS, 2, quarter_rows // 2, WIDE), jnp.float32),
        [buffer(), buffer(jnp.bfloat16), buffer(), pltpu.SemaphoreType.DMA((PARTS, 3))],
        flops=cells * 1024, moved=cells * 11,
    )

    def along_z(value, s):
        return lax.ppermute(value, "fsdp", [(i, i ^ s) for i in range(shards)])

    def along_rep(value, s):
        return lax.ppermute(value, "rep", [(i, i ^ s) for i in range(replicas)])

    quarter = partial[0] + along_z(partial[1], 1) + along_z(partial[2], 2) + along_z(partial[3], 3)
    next1, next2 = along_z(quarter, 1), along_z(quarter, 2)
    next3 = along_z(next2, 1)
    total = quarter[0] + along_rep(quarter[1], 1)
    total = total + along_rep(total, 2)
    total = total + along_rep(total, 4) + along_rep(total, 8) + along_rep(total, 12)
    next1, next2, next3, total = lax.optimization_barrier((next1, next2, next3, total))
    own_pieces = [total] + [along_z(total, s) for s in range(1, PARTS)]

    new_error = call(
        error_kernel, "error",
        (quarter, next1, next2, next3, in_hbm(base_params), in_hbm(local_params), in_hbm(error_buffer), col_inv, rows_inv),
        [VMEM] * PARTS + [HBM, HBM, HBM, VMEM, VMEM],
        HBM, f32(1, rows, width),
        [buffer(), buffer(jnp.bfloat16), buffer(), buffer(), pltpu.SemaphoreType.DMA((PARTS, 4))],
        flops=cells * 1024, moved=cells * 15,
    )
    *own_pieces, new_error = lax.optimization_barrier((*own_pieces, new_error))
    own = jnp.stack(own_pieces)
    other = along_rep(own, 1)
    new_base, new_momentum = call(
        functools.partial(update_kernel, replicas), "update",
        (own, other, base_params, momentum, col_inv, rows_inv),
        [VMEM] * 6,
        [HBM, HBM], [f32(rows, width), f32(rows, width)],
        [buffer(), buffer(), pltpu.SemaphoreType.DMA((PARTS, 2))],
        flops=cells * 1024, moved=cells * 16,
    )
    return (new_base, new_error, new_momentum)


def solution(mesh):
    in_specs = (P("rep", "fsdp", None), P("fsdp", None), P("rep", "fsdp", None), P("fsdp", None))
    out_specs = (P("fsdp", None), P("rep", "fsdp", None), P("fsdp", None))
    return jax.shard_map(local, mesh=mesh, in_specs=in_specs, out_specs=out_specs, check_vma=False)
```

time: 316 us -> 51.7 us (0.16)
  waiting for transfers between devices: 208 us -> 21.5 us
  local copies, waits for them, and re-layouts: 32.3 us -> 1.76 us
  matrix products: 24.4 us -> 0 us
  between operations: 14.1 us -> 0.76 us
  starting transfers between devices: 28.1 us -> 18.1 us
  Pallas kernels: 0 us -> 9.38 us
  other arithmetic: 8.63 us -> 0.07 us
    psum x1 -> x0, waiting for transfers between devices: 126 us -> none  [local(): summed = lax.psum(coefficients, 'rep')]
    all_to_all x3 -> x0, waiting for transfers between devices: 81.4 us -> none  [the longest x1 43.2 us: local(): lax.all_to_all(pseudo_grad, 'fsdp', split_axis=1, concat_axis=0, tiled=True)]
    all_to_all x3 -> x0, starting transfers between devices: 28 us -> none  [the longest x1 11.7 us: local(): lax.all_to_all(pseudo_grad, 'fsdp', split_axis=1, concat_axis=0, tiled=True)]
    dot_general x6 -> x0, matrix products: 24.4 us -> none  [the longest x4 13.8 us: inverse_band(): jnp.einsum('ka,ikjl,lb->iajb', lowband, blocks, lowband, precision=lax.Pr...]
    ppermute x0 -> x15, waiting for transfers between devices: none -> 21.5 us  [the longest x9 17.4 us: along_z(): return lax.ppermute(value, 'fsdp', [(i, i ^ s) for i in range(shards)])]
    ppermute x0 -> x15, starting transfers between devices: none -> 18.1 us  [the longest x9 10 us: along_z(): return lax.ppermute(value, 'fsdp', [(i, i ^ s) for i in range(shards)])]
    all_to_all x4 -> x0, local copies, waits for them, and re-layouts: 10.1 us -> none  [the longest x2 6.41 us: local(): lax.all_to_all(outer_cols, 'fsdp', split_axis=0, concat_axis=1, tiled=True)]
    pallas_call x0 -> x3, Pallas kernels: none -> 9.38 us  [call(): pl.pallas_call(kernel, in_specs=in_specs, out_specs=out_specs, out_shape=...]
  transfers between devices with their start and end apart: 4 -> 15, of which waited for: 3 -> 9; matrix products, arithmetic and copies ran while one was open for 6% -> 0% of each run, Pallas kernels for 0% -> 7%
where the time goes in v1:
time: 51.7 us; the launch traced here: 51.6 us
  waiting for transfers between devices  21.5 us (42%)
  starting transfers between devices  18.1 us (35%)
  Pallas kernels  9.38 us (18%)
  local copies, waits for them, and re-layouts  1.76 us (3%)
  between operations  0.76 us (1%)
    ppermute x9, waiting for transfers between devices, along_z(): return lax.ppermute(value, 'fsdp', [(i, i ^ s) for i in range(shards)])  17.4 us
    ppermute x9, starting transfers between devices, along_z(): return lax.ppermute(value, 'fsdp', [(i, i ^ s) for i in range(shards)])  10 us
    pallas_call x3, Pallas kernels, call(): pl.pallas_call(kernel, in_specs=in_specs, out_specs=out_specs, out_shape=...  9.38 us
    ppermute x6, starting transfers between devices, along_rep(): return lax.ppermute(value, 'rep', [(i, i ^ s) for i in range(replicas)])  8.05 us
    ppermute x6, waiting for transfers between devices, along_rep(): return lax.ppermute(value, 'rep', [(i, i ^ s) for i in range(replicas)])  4.15 us
    unnamed x12, local copies, waits for them, and re-layouts  1.73 us
  transfers between devices with their start and end apart: 15, of which 9 were waited for; matrix products, arithmetic and copies ran while one was open for 0% of the time, Pallas kernels for 7%

profile of v1, /device:TPU:1, one launch (start us, length us, event | category | flops | bytes accessed | tf_op | source)
XLA Modules:
  0.0 51.6 jit_solution(11193977538884944642)
XLA Ops:
  0.6 0.0 copy-start.3
  0.6 0.9 %copy-done.3 = bf16[512,256]{1,0:T(8,128)(2,1)S(1)} copy-done((bf16[512,256]{1,0:T(8,128)(2,1)S(1)}, bf16[512,256]{1,0:T(8,128)(2,1)}, u32[]{:S(2)}) %copy-start.3) | copy-done | bytes 262168
  1.6 0.8 %copy-done.5 = f32[4,16,16]{2,1,0:T(8,128)S(1)} copy-done((f32[4,16,16]{2,1,0:T(8,128)S(1)}, f32[4,16,16]{2,1,0:T(8,128)}, u32[]{:S(2)}) %copy-start.5) | copy-done | bytes 4120
  2.3 3.3 %forward.1 = f32[4,2,112,128]{3,2,1,0:T(8,128)S(1)} custom-call(f32[16,28672]{1,0:T(8,128)} %base.5, bf16[1,16,28672]{2,1,0:T(8,128)(2,1)} %local.3, f32[1,16,28672]{2,1,0:T(8,128)} %err.3, bf16[512,256]{1,0:T(8,128)(2,1)S(1)} %copy-done.3, f32[4,16,16]{2,1,0:T(8,128)S(1)} %copy-done.5), custom_call_target="tpu_custom_call" | custom-call | flops 469762048 | bytes 5046272 | tf_op jit(solution)/shard_map/forward/pallas_call | solution.py:175
  5.6 0.0 copy-start.1
  5.6 0.0 copy-start.4
  5.7 2.6 %collective-permute-start = (f32[2,112,128]{2,1,0:T(8,128)S(1)}, f32[2,112,128]{2,1,0:T(8,128)S(1)}, u32[]{:S(2)}, u32[]{:S(2)}) collective-permute-start(f32[2,112,128]{2,1,0:T(8,128)S(1)} %get-tuple-element.25), channel_id=1, source_target_pairs={{0,1},{1,0},{2,3},{3,2},{4,5},{5,4},{6,7},{7,6},{8,9},{9,8},{10,11... | collective-permute-start | bytes 344072 | tf_op jit(solution)/shard_map/ppermute | solution.py:211
  8.2 2.8 %collective-permute-start.2 = (f32[2,112,128]{2,1,0:T(8,128)S(1)}, f32[2,112,128]{2,1,0:T(8,128)S(1)}, u32[]{:S(2)}, u32[]{:S(2)}) collective-permute-start(f32[2,112,128]{2,1,0:T(8,128)S(1)} %get-tuple-element.26), channel_id=1, source_target_pairs={{0,3},{1,2},{2,1},{3,0},{4,7},{5,6},{6,5},{7,4},{8,11},{9,10},{10,... | collective-permute-start | bytes 344072 | tf_op jit(solution)/shard_map/ppermute | solution.py:211
  11.1 0.2 collective-permute-start.1
  11.2 0.0 collective-permute-done
  11.2 4.9 %collective-permute-done.2 = f32[2,112,128]{2,1,0:T(8,128)S(1)} collective-permute-done((f32[2,112,128]{2,1,0:T(8,128)S(1)}, f32[2,112,128]{2,1,0:T(8,128)S(1)}, u32[]{:S(2)}, u32[]{:S(2)}) %collective-permute-start.2) | collective-permute-done | bytes 114720 | tf_op jit(solution)/shard_map/ppermute | solution.py:211
  16.2 5.4 %collective-permute-done.1 = f32[2,112,128]{2,1,0:T(8,128)S(1)} collective-permute-done((f32[2,112,128]{2,1,0:T(8,128)S(1)}, f32[2,112,128]{2,1,0:T(8,128)S(1)}, u32[]{:S(2)}, u32[]{:S(2)}) %collective-permute-start.1) | collective-permute-done | bytes 114720 | tf_op jit(solution)/shard_map/ppermute | solution.py:211
  21.6 1.2 %collective-permute-start.6 = (f32[112,128]{1,0:T(8,128)S(1)}, f32[112,128]{1,0:T(8,128)S(1)}, u32[]{:S(2)}, u32[]{:S(2)}) collective-permute-start(f32[112,128]{1,0:T(8,128)S(1)} %slice_bitcast_fusion.4), channel_id=1, source_target_pairs={{0,16},{16,0},{32,48},{48,32},{64,80},{80,64},{96,112},{112,96},{1... | collective-permute-start | bytes 172040 | tf_op jit(solution)/shard_map/ppermute | solution.py:214
  22.8 0.9 %collective-permute-done.6 = f32[112,128]{1,0:T(8,128)S(1)} collective-permute-done((f32[112,128]{1,0:T(8,128)S(1)}, f32[112,128]{1,0:T(8,128)S(1)}, u32[]{:S(2)}, u32[]{:S(2)}) %collective-permute-start.6) | collective-permute-done | bytes 57376 | tf_op jit(solution)/shard_map/ppermute | solution.py:214
  23.7 1.3 %collective-permute-start.7 = (f32[112,128]{1,0:T(8,128)S(1)}, f32[112,128]{1,0:T(8,128)S(1)}, u32[]{:S(2)}, u32[]{:S(2)}) collective-permute-start(f32[112,128]{1,0:T(8,128)S(1)} %fusion.3), channel_id=1, source_target_pairs={{0,32},{16,48},{32,0},{48,16},{64,96},{80,112},{96,64},{112,80},{1... | collective-permute-start | bytes 172040 | tf_op jit(solution)/shard_map/ppermute | solution.py:214
  25.1 1.7 %collective-permute-done.7 = f32[112,128]{1,0:T(8,128)S(1)} collective-permute-done((f32[112,128]{1,0:T(8,128)S(1)}, f32[112,128]{1,0:T(8,128)S(1)}, u32[]{:S(2)}, u32[]{:S(2)}) %collective-permute-start.7) | collective-permute-done | bytes 57376 | tf_op jit(solution)/shard_map/ppermute | solution.py:214
  26.8 2.6 %collective-permute-start.10 = (f32[112,128]{1,0:T(8,128)S(1)}, f32[112,128]{1,0:T(8,128)S(1)}, u32[]{:S(2)}, u32[]{:S(2)}) collective-permute-start(f32[112,128]{1,0:T(8,128)S(1)} %add.28), channel_id=1, source_target_pairs={{0,192},{16,208},{32,224},{48,240},{64,128},{80,144},{96,160},{112... | collective-permute-start | bytes 172040 | tf_op jit(solution)/shard_map/ppermute | solution.py:214
  29.4 0.5 %collective-permute-start.9 = (f32[112,128]{1,0:T(8,128)S(1)}, f32[112,128]{1,0:T(8,128)S(1)}, u32[]{:S(2)}, u32[]{:S(2)}) collective-permute-start(f32[112,128]{1,0:T(8,128)S(1)} %add.28), channel_id=1, source_target_pairs={{0,128},{16,144},{32,160},{48,176},{64,192},{80,208},{96,224},{112... | collective-permute-start | bytes 172040 | tf_op jit(solution)/shard_map/ppermute | solution.py:214
  29.9 0.3 collective-permute-start.8
  30.2 0.9 %collective-permute-start.3 = (f32[2,112,128]{2,1,0:T(8,128)S(1)}, f32[2,112,128]{2,1,0:T(8,128)S(1)}, u32[]{:S(2)}, u32[]{:S(2)}) collective-permute-start(f32[2,112,128]{2,1,0:T(8,128)S(1)} %fusion.2.k0), channel_id=1, source_target_pairs={{0,1},{1,0},{2,3},{3,2},{4,5},{5,4},{6,7},{7,6},{8,9},{9,8},{10,11... | collective-permute-start | bytes 344072 | tf_op jit(solution)/shard_map/ppermute | solution.py:211
  31.1 2.4 %collective-permute-done.4.k2 = f32[2,112,128]{2,1,0:T(8,128)S(1)} collective-permute-done((f32[2,112,128]{2,1,0:T(8,128)S(1)}, f32[2,112,128]{2,1,0:T(8,128)S(1)}, u32[]{:S(2)}, u32[]{:S(2)}) %collective-permute-start.4) | collective-permute-done | bytes 114720 | tf_op jit(solution)/shard_map/ppermute | solution.py:211
  33.5 0.4 collective-permute-done.9
  33.9 0.0 copy-start
  34.0 0.0 copy-start.2
  34.0 0.6 %collective-permute-done.3.k1 = f32[2,112,128]{2,1,0:T(8,128)S(1)} collective-permute-done((f32[2,112,128]{2,1,0:T(8,128)S(1)}, f32[2,112,128]{2,1,0:T(8,128)S(1)}, u32[]{:S(2)}, u32[]{:S(2)}) %collective-permute-start.3) | collective-permute-done | bytes 114720 | tf_op jit(solution)/shard_map/ppermute | solution.py:211
  34.5 4.1 %collective-permute-done.5.k3 = f32[2,112,128]{2,1,0:T(8,128)S(1)} collective-permute-done((f32[2,112,128]{2,1,0:T(8,128)S(1)}, f32[2,112,128]{2,1,0:T(8,128)S(1)}, u32[]{:S(2)}, u32[]{:S(2)}) %collective-permute-start.5) | collective-permute-done | bytes 114720 | tf_op jit(solution)/shard_map/ppermute | solution.py:211
  38.6 1.3 %collective-permute-start.12 = (f32[112,128]{1,0:T(8,128)S(1)}, f32[112,128]{1,0:T(8,128)S(1)}, u32[]{:S(2)}, u32[]{:S(2)}) collective-permute-start(f32[112,128]{1,0:T(8,128)S(1)} %add_add_fusion), channel_id=1, source_target_pairs={{0,2},{1,3},{2,0},{3,1},{4,6},{5,7},{6,4},{7,5},{8,10},{9,11},{10,... | collective-permute-start | bytes 172040 | tf_op jit(solution)/shard_map/ppermute | solution.py:211
  39.9 2.3 %collective-permute-start.11 = (f32[112,128]{1,0:T(8,128)S(1)}, f32[112,128]{1,0:T(8,128)S(1)}, u32[]{:S(2)}, u32[]{:S(2)}) collective-permute-start(f32[112,128]{1,0:T(8,128)S(1)} %add_add_fusion), channel_id=1, source_target_pairs={{0,1},{1,0},{2,3},{3,2},{4,5},{5,4},{6,7},{7,6},{8,9},{9,8},{10,11... | collective-permute-start | bytes 172040 | tf_op jit(solution)/shard_map/ppermute | solution.py:211
  42.1 3.6 %error.1 = f32[1,16,28672]{2,1,0:T(8,128)} custom-call(f32[2,112,128]{2,1,0:T(8,128)S(1)} %fusion.2.k0, f32[2,112,128]{2,1,0:T(8,128)S(1)} %collective-permute-done.3.k1, f32[2,112,128]{2,1,0:T(8,128)S(1)} %collective-permute-done.4.k2, f32[2,112,128]{2,1,0:T(8,128)S(1)} %collective-permute-done.5.k3, f32[16,28672]{1,0:T(8,128)} %base.5, ...), custom_call_target="tpu_custom_call" | custom-call | flops 469762048 | bytes 6881280 | tf_op jit(solution)/shard_map/error/pallas_call | solution.py:175
  45.8 2.1 %collective-permute-start.14 = (f32[4,112,128]{2,1,0:T(8,128)S(1)}, f32[4,112,128]{2,1,0:T(8,128)S(1)}, u32[]{:S(2)}, u32[]{:S(2)}) collective-permute-start(f32[4,112,128]{2,1,0:T(8,128)S(1)} %pad_maximum_fusion.own), channel_id=1, source_target_pairs={{0,16},{16,0},{32,48},{48,32},{64,80},{80,64},{96,112},{112,96},{1... | collective-permute-start | bytes 688136 | tf_op jit(solution)/shard_map/ppermute | solution.py:214
  47.9 1.1 %collective-permute-done.14.other = f32[4,112,128]{2,1,0:T(8,128)S(1)} collective-permute-done((f32[4,112,128]{2,1,0:T(8,128)S(1)}, f32[4,112,128]{2,1,0:T(8,128)S(1)}, u32[]{:S(2)}, u32[]{:S(2)}) %collective-permute-start.14) | collective-permute-done | bytes 229408 | tf_op jit(solution)/shard_map/ppermute | solution.py:214
  49.1 2.5 %update.1 = (f32[16,28672]{1,0:T(8,128)}, f32[16,28672]{1,0:T(8,128)}) custom-call(f32[4,112,128]{2,1,0:T(8,128)S(1)} %pad_maximum_fusion.own, f32[4,112,128]{2,1,0:T(8,128)S(1)} %collective-permute-done.14.other, f32[16,28672]{1,0:T(8,128)S(1)} %copy-done, f32[16,28672]{1,0:T(8,128)S(1)} %copy-done.2, bf16[2,256,512]{2,1,0:T(8,128)(2,1)S(1)} %copy-done.1, ...), custom_call_target="tpu_custom_call" | custom-call | flops 469762048 | bytes 7340032 | tf_op jit(solution)/shard_map/update/pallas_call | solution.py:175
  (20 shorter events, 0.1 us)
Async XLA Ops:
  0.6 1.0 %copy-start.3 = (bf16[512,256]{1,0:T(8,128)(2,1)S(1)}, bf16[512,256]{1,0:T(8,128)(2,1)}, u32[]{:S(2)}) copy-start(bf16[512,256]{1,0:T(8,128)(2,1)} %constant.8.clone.col) | copy-start | bytes 786436
  1.6 0.8 %copy-start.5 = (f32[4,16,16]{2,1,0:T(8,128)S(1)}, f32[4,16,16]{2,1,0:T(8,128)}, u32[]{:S(2)}) copy-start(f32[4,16,16]{2,1,0:T(8,128)} %constant.10.clone.rows) | copy-start | bytes 12292
  5.6 36.5 %copy-start.1 = (bf16[2,256,512]{2,1,0:T(8,128)(2,1)S(1)}, bf16[2,256,512]{2,1,0:T(8,128)(2,1)}, u32[]{:S(2)}) copy-start(bf16[2,256,512]{2,1,0:T(8,128)(2,1)} %constant.9.clone.col) | copy-start | bytes 1572868
  5.6 36.5 %copy-start.4 = (f32[4,16,16]{2,1,0:T(8,128)S(1)}, f32[4,16,16]{2,1,0:T(8,128)}, u32[]{:S(2)}) copy-start(f32[4,16,16]{2,1,0:T(8,128)} %constant.11.clone.rows) | copy-start | bytes 12292
  5.7 5.6 %collective-permute-start = (f32[2,112,128]{2,1,0:T(8,128)S(1)}, f32[2,112,128]{2,1,0:T(8,128)S(1)}, u32[]{:S(2)}, u32[]{:S(2)}) collective-permute-start(f32[2,112,128]{2,1,0:T(8,128)S(1)} %get-tuple-element.25), channel_id=1, source_target_pairs={{0,1},{1,0},{2,3},{3,2},{4,5},{5,4},{6,7},{7,6},{8,9},{9,8},{10,11... | collective-permute-start | bytes 344072 | tf_op jit(solution)/shard_map/ppermute | solution.py:211
  8.2 7.9 %collective-permute-start.2 = (f32[2,112,128]{2,1,0:T(8,128)S(1)}, f32[2,112,128]{2,1,0:T(8,128)S(1)}, u32[]{:S(2)}, u32[]{:S(2)}) collective-permute-start(f32[2,112,128]{2,1,0:T(8,128)S(1)} %get-tuple-element.26), channel_id=1, source_target_pairs={{0,3},{1,2},{2,1},{3,0},{4,7},{5,6},{6,5},{7,4},{8,11},{9,10},{10,... | collective-permute-start | bytes 344072 | tf_op jit(solution)/shard_map/ppermute | solution.py:211
  11.1 10.5 %collective-permute-start.1 = (f32[2,112,128]{2,1,0:T(8,128)S(1)}, f32[2,112,128]{2,1,0:T(8,128)S(1)}, u32[]{:S(2)}, u32[]{:S(2)}) collective-permute-start(f32[2,112,128]{2,1,0:T(8,128)S(1)} %get-tuple-element.27), channel_id=1, source_target_pairs={{0,2},{1,3},{2,0},{3,1},{4,6},{5,7},{6,4},{7,5},{8,10},{9,11},{10,... | collective-permute-start | bytes 344072 | tf_op jit(solution)/shard_map/ppermute | solution.py:211
  21.6 2.1 %collective-permute-start.6 = (f32[112,128]{1,0:T(8,128)S(1)}, f32[112,128]{1,0:T(8,128)S(1)}, u32[]{:S(2)}, u32[]{:S(2)}) collective-permute-start(f32[112,128]{1,0:T(8,128)S(1)} %slice_bitcast_fusion.4), channel_id=1, source_target_pairs={{0,16},{16,0},{32,48},{48,32},{64,80},{80,64},{96,112},{112,96},{1... | collective-permute-start | bytes 172040 | tf_op jit(solution)/shard_map/ppermute | solution.py:214
  23.7 3.1 %collective-permute-start.7 = (f32[112,128]{1,0:T(8,128)S(1)}, f32[112,128]{1,0:T(8,128)S(1)}, u32[]{:S(2)}, u32[]{:S(2)}) collective-permute-start(f32[112,128]{1,0:T(8,128)S(1)} %fusion.3), channel_id=1, source_target_pairs={{0,32},{16,48},{32,0},{48,16},{64,96},{80,112},{96,64},{112,80},{1... | collective-permute-start | bytes 172040 | tf_op jit(solution)/shard_map/ppermute | solution.py:214
  25.1 8.4 %collective-permute-start.4 = (f32[2,112,128]{2,1,0:T(8,128)S(1)}, f32[2,112,128]{2,1,0:T(8,128)S(1)}, u32[]{:S(2)}, u32[]{:S(2)}) collective-permute-start(f32[2,112,128]{2,1,0:T(8,128)S(1)} %fusion.2.k0), channel_id=1, source_target_pairs={{0,2},{1,3},{2,0},{3,1},{4,6},{5,7},{6,4},{7,5},{8,10},{9,11},{10,... | collective-permute-start | bytes 344072 | tf_op jit(solution)/shard_map/ppermute | solution.py:211
  26.8 6.7 %collective-permute-start.10 = (f32[112,128]{1,0:T(8,128)S(1)}, f32[112,128]{1,0:T(8,128)S(1)}, u32[]{:S(2)}, u32[]{:S(2)}) collective-permute-start(f32[112,128]{1,0:T(8,128)S(1)} %add.28), channel_id=1, source_target_pairs={{0,192},{16,208},{32,224},{48,240},{64,128},{80,144},{96,160},{112... | collective-permute-start | bytes 172040 | tf_op jit(solution)/shard_map/ppermute | solution.py:214
  29.4 4.5 %collective-permute-start.9 = (f32[112,128]{1,0:T(8,128)S(1)}, f32[112,128]{1,0:T(8,128)S(1)}, u32[]{:S(2)}, u32[]{:S(2)}) collective-permute-start(f32[112,128]{1,0:T(8,128)S(1)} %add.28), channel_id=1, source_target_pairs={{0,128},{16,144},{32,160},{48,176},{64,192},{80,208},{96,224},{112... | collective-permute-start | bytes 172040 | tf_op jit(solution)/shard_map/ppermute | solution.py:214
  29.9 4.0 %collective-permute-start.8 = (f32[112,128]{1,0:T(8,128)S(1)}, f32[112,128]{1,0:T(8,128)S(1)}, u32[]{:S(2)}, u32[]{:S(2)}) collective-permute-start(f32[112,128]{1,0:T(8,128)S(1)} %add.28), channel_id=1, source_target_pairs={{0,64},{16,80},{32,96},{48,112},{64,0},{80,16},{96,32},{112,48},{1... | collective-permute-start | bytes 172040 | tf_op jit(solution)/shard_map/ppermute | solution.py:214
  30.2 4.4 %collective-permute-start.3 = (f32[2,112,128]{2,1,0:T(8,128)S(1)}, f32[2,112,128]{2,1,0:T(8,128)S(1)}, u32[]{:S(2)}, u32[]{:S(2)}) collective-permute-start(f32[2,112,128]{2,1,0:T(8,128)S(1)} %fusion.2.k0), channel_id=1, source_target_pairs={{0,1},{1,0},{2,3},{3,2},{4,5},{5,4},{6,7},{7,6},{8,9},{9,8},{10,11... | collective-permute-start | bytes 344072 | tf_op jit(solution)/shard_map/ppermute | solution.py:211
  33.5 5.1 %collective-permute-start.5 = (f32[2,112,128]{2,1,0:T(8,128)S(1)}, f32[2,112,128]{2,1,0:T(8,128)S(1)}, u32[]{:S(2)}, u32[]{:S(2)}) collective-permute-start(f32[2,112,128]{2,1,0:T(8,128)S(1)} %collective-permute-done.4.k2), channel_id=1, source_target_pairs={{0,1},{1,0},{2,3},{3,2},{4,5},{5,4},{6,7},{7,6},{8,9},{9,8},{10,11... | collective-permute-start | bytes 344072 | tf_op jit(solution)/shard_map/ppermute | solution.py:211
  33.9 15.1 %copy-start = (f32[16,28672]{1,0:T(8,128)S(1)}, f32[16,28672]{1,0:T(8,128)}, u32[]{:S(2)}) copy-start(f32[16,28672]{1,0:T(8,128)} %base.5) | copy-start | bytes 5505028
  34.0 15.1 %copy-start.2 = (f32[16,28672]{1,0:T(8,128)S(1)}, f32[16,28672]{1,0:T(8,128)}, u32[]{:S(2)}) copy-start(f32[16,28672]{1,0:T(8,128)} %mom.1) | copy-start | bytes 5505028
  38.6 7.2 %collective-permute-start.13 = (f32[112,128]{1,0:T(8,128)S(1)}, f32[112,128]{1,0:T(8,128)S(1)}, u32[]{:S(2)}, u32[]{:S(2)}) collective-permute-start(f32[112,128]{1,0:T(8,128)S(1)} %add_add_fusion), channel_id=1, source_target_pairs={{0,3},{1,2},{2,1},{3,0},{4,7},{5,6},{6,5},{7,4},{8,11},{9,10},{10,... | collective-permute-start | bytes 172040 | tf_op jit(solution)/shard_map/ppermute | solution.py:211
  38.6 7.2 %collective-permute-start.12 = (f32[112,128]{1,0:T(8,128)S(1)}, f32[112,128]{1,0:T(8,128)S(1)}, u32[]{:S(2)}, u32[]{:S(2)}) collective-permute-start(f32[112,128]{1,0:T(8,128)S(1)} %add_add_fusion), channel_id=1, source_target_pairs={{0,2},{1,3},{2,0},{3,1},{4,6},{5,7},{6,4},{7,5},{8,10},{9,11},{10,... | collective-permute-start | bytes 172040 | tf_op jit(solution)/shard_map/ppermute | solution.py:211
  39.9 5.9 %collective-permute-start.11 = (f32[112,128]{1,0:T(8,128)S(1)}, f32[112,128]{1,0:T(8,128)S(1)}, u32[]{:S(2)}, u32[]{:S(2)}) collective-permute-start(f32[112,128]{1,0:T(8,128)S(1)} %add_add_fusion), channel_id=1, source_target_pairs={{0,1},{1,0},{2,3},{3,2},{4,5},{5,4},{6,7},{7,6},{8,9},{9,8},{10,11... | collective-permute-start | bytes 172040 | tf_op jit(solution)/shard_map/ppermute | solution.py:211
  45.8 3.2 %collective-permute-start.14 = (f32[4,112,128]{2,1,0:T(8,128)S(1)}, f32[4,112,128]{2,1,0:T(8,128)S(1)}, u32[]{:S(2)}, u32[]{:S(2)}) collective-permute-start(f32[4,112,128]{2,1,0:T(8,128)S(1)} %pad_maximum_fusion.own), channel_id=1, source_target_pairs={{0,16},{16,0},{32,48},{48,32},{64,80},{80,64},{96,112},{112,96},{1... | collective-permute-start | bytes 688136 | tf_op jit(solution)/shard_map/ppermute | solution.py:214

commit v2 on v1

--- a/solution.py
+++ b/solution.py
@@ -76,36 +76,41 @@
     return pl.ds(pl.multiple_of((part ^ s) * size, GROUP), size)
 
 
-def forward_kernel(base, local, err, col, rows, out, base_v, local_v, err_v, sems):
+def forward_kernel(steps, base, local, err, col, rows, out, base_v, local_v, err_v, col_v, rows_v, sems, table_sems):
     part, core = position()
     width = base.shape[1]
+    tables = (
+        pltpu.make_async_copy(col, col_v, table_sems.at[0]),
+        pltpu.make_async_copy(rows.at[part], rows_v, table_sems.at[1]),
+    )
     copies = []
-    for s in range(PARTS):
+    for i, s in enumerate(steps):
         cols = quarter_cols(part, s, width)
         copies.append(
             [
-                pltpu.make_async_copy(base.at[:, cols], base_v.at[s], sems.at[s, 0]),
-                pltpu.make_async_copy(err.at[0, :, cols], err_v.at[s], sems.at[s, 1]),
-                pltpu.make_async_copy(local.at[0, :, cols], local_v.at[s], sems.at[s, 2]),
+                pltpu.make_async_copy(base.at[:, cols], base_v.at[i], sems.at[i, 0]),
+                pltpu.make_async_copy(err.at[0, :, cols], err_v.at[i], sems.at[i, 1]),
+                pltpu.make_async_copy(local.at[0, :, cols], local_v.at[i], sems.at[i, 2]),
             ]
         )
-    for step in copies:
-        for copy in step:
-            copy.start()
-    table = rows[part]
-    for s in range(PARTS):
-        for copy in copies[s]:
+    for copy in (*copies[0], *tables, *(copy for step in copies[1:] for copy in step)):
+        copy.start()
+    for i in range(len(steps)):
+        for copy in copies[i]:
             copy.wait()
-        field = base_v[s] - local_v[s].astype(jnp.float32) + err_v[s]
+        if i == 0:
+            for copy in tables:
+                copy.wait()
+        field = base_v[i] - local_v[i].astype(jnp.float32) + err_v[i]
         groups = field.shape[1] // GROUP
         stacked = jnp.concatenate([field[:, GROUP * g : GROUP * (g + 1)] for g in range(groups)], axis=0)
         count = stacked.shape[0]
-        both = dot(jnp.concatenate(split(stacked), axis=0), col[...])
+        both = dot(jnp.concatenate(split(stacked), axis=0), col_v[...])
         both = both[:, :WIDE] + both[:, WIDE:]
-        coeffs = apply_rows(table, both[:count] + both[count:])
+        coeffs = apply_rows(rows_v[...], both[:count] + both[count:])
         half = count // 2
-        out[s, core] = coeffs[:half]
-        out[s, 1 - core] = coeffs[half:]
+        out[i, core] = coeffs[:half]
+        out[i, 1 - core] = coeffs[half:]
 
 
 def inverse_rows(table, col, coeffs):
@@ -145,25 +150,25 @@
         write.wait()
 
 
-def update_kernel(replicas, own, other, base, mom, col, rows, base_out, mom_out, base_w, mom_w, sems):
+def update_kernel(replicas, half, mean, base, mom, col, rows, *refs):
+    base_out, mom_out, base_w, mom_w, sems = refs[-5:]
     part, core = position()
     width = base.shape[1]
     table = rows[part]
+    size = width // PARTS // 2
+    here = core if half == 0 else 1 - core
     writes = []
     for s in range(PARTS):
-        cols = quarter_cols(part, s, width)
-        both = jnp.stack([own[s], other[s]]) * (1.0 / replicas)
-        first = jnp.where(core == 0, both[0], both[1])
-        second = jnp.where(core == 0, both[1], both[0])
-        outer = inverse_rows(table, col, jnp.concatenate([first, second], axis=0))
-        size = width // PARTS
+        start = ((part ^ s) * 2 + here) * size
+        outer = inverse_rows(table, col, mean[s] * (1.0 / replicas))
         for g in range(size // GROUP):
             at = slice(GROUP * g, GROUP * (g + 1))
-            src = pl.ds(pl.multiple_of((part ^ s) * size + GROUP * g, GROUP), GROUP)
+            src = pl.ds(pl.multiple_of(start + GROUP * g, GROUP), GROUP)
             grad = outer[ROWS * g : ROWS * (g + 1)]
             new_momentum = OUTER_BETA * mom[:, src] + grad
             mom_w[s, :, at] = new_momentum
             base_w[s, :, at] = base[:, src] - OUTER_RATE * (grad + OUTER_BETA * new_momentum)
+        cols = pl.ds(pl.multiple_of(start, GROUP), size)
         for i, (src, dst) in enumerate(((base_w, base_out), (mom_w, mom_out))):
             writes.append(pltpu.make_async_copy(src.at[s], dst.at[:, cols], sems.at[s, i]))
             writes[-1].start()
@@ -171,7 +176,7 @@
         write.wait()
 
 
-def call(kernel, name, inputs, in_specs, out_specs, out_shape, scratch, flops, moved):
+def call(kernel, name, inputs, in_specs, out_specs, out_shape, scratch, flops, moved, aliases={}):
     return pl.pallas_call(
         kernel,
         in_specs=in_specs,
@@ -180,6 +185,7 @@
         scratch_shapes=scratch,
         compiler_params=pltpu.CompilerParams(vmem_limit_bytes=VMEM_LIMIT),
         cost_estimate=pl.CostEstimate(flops=flops, bytes_accessed=moved, transcendentals=0),
+        input_output_aliases=aliases,
         name=name,
     )(*inputs)
 
@@ -198,29 +204,41 @@
     buffer = lambda dtype=jnp.float32: pltpu.VMEM((PARTS, rows, width // PARTS), dtype)
     cells = rows * width
 
-    partial = call(
-        forward_kernel, "forward",
-        (in_hbm(base_params), in_hbm(local_params), in_hbm(error_buffer), col_fwd, rows_fwd),
-        [HBM, HBM, HBM, VMEM, VMEM],
-        VMEM, pltpu.VMEM((PARTS, 2, quarter_rows // 2, WIDE), jnp.float32),
-        [buffer(), buffer(jnp.bfloat16), buffer(), pltpu.SemaphoreType.DMA((PARTS, 3))],
-        flops=cells * 1024, moved=cells * 11,
-    )
-
-    def along_z(value, s):
-        return lax.ppermute(value, "fsdp", [(i, i ^ s) for i in range(shards)])
-
-    def along_rep(value, s):
-        return lax.ppermute(value, "rep", [(i, i ^ s) for i in range(replicas)])
-
-    quarter = partial[0] + along_z(partial[1], 1) + along_z(partial[2], 2) + along_z(partial[3], 3)
-    next1, next2 = along_z(quarter, 1), along_z(quarter, 2)
-    next3 = along_z(next2, 1)
-    total = quarter[0] + along_rep(quarter[1], 1)
-    total = total + along_rep(total, 2)
-    total = total + along_rep(total, 4) + along_rep(total, 8) + along_rep(total, 12)
-    next1, next2, next3, total = lax.optimization_barrier((next1, next2, next3, total))
-    own_pieces = [total] + [along_z(total, s) for s in range(1, PARTS)]
+    def forward(*steps):
+        count = len(steps)
+        pair = lambda dtype=jnp.float32: pltpu.VMEM((count, rows, width // PARTS), dtype)
+        coeffs = call(
+            functools.partial(forward_kernel, steps), "forward",
+            [in_hbm(v) for v in (base_params, local_params, error_buffer, col_fwd, rows_fwd)],
+            [HBM] * 5,
+            VMEM, pltpu.VMEM((count, 2, quarter_rows // 2, WIDE), jnp.float32),
+            [pair(), pair(jnp.bfloat16), pair(), pltpu.VMEM(col_fwd.shape, jnp.bfloat16), pltpu.VMEM(rows_fwd.shape[1:], jnp.float32),
+             pltpu.SemaphoreType.DMA((count, 3)), pltpu.SemaphoreType.DMA((2,))],
+            flops=cells * 256 * count, moved=cells * 11 * count // PARTS,
+        )
+        return tuple(coeffs[i] for i in range(count))
+
+    def along_z(value, s, name):
+        with jax.named_scope(f"{name}{s}"):
+            return lax.ppermute(value, "fsdp", [(i, i ^ s) for i in range(shards)])
+
+    def along_rep(value, s, name):
+        with jax.named_scope(f"{name}{s}"):
+            return lax.ppermute(value, "rep", [(i, i ^ s) for i in range(replicas)])
+
+    (part2,) = forward(2)
+    far2 = along_z(part2, 2, "far")
+    part3, part1, part0 = forward(3, 1, 0)
+    near1 = along_z(part1, 1, "near")
+    far3 = along_z(part3, 3, "far")
+    quarter = part0 + near1 + far3 + far2
+    total = quarter[0] + along_rep(quarter[1], 1, "core")
+    total = total + along_rep(total, 2, "ylo")
+    x12, x4, x8 = (along_rep(total, s, "x") for s in (12, 4, 8))
+    next1, next3, next2 = (along_z(quarter, s, "next") for s in (1, 3, 2))
+    next1, next2, next3, x8 = lax.optimization_barrier((next1, next2, next3, x8))
+    total = total + x8 + x4 + x12
+    own_pieces = [total] + [along_z(total, s, "mean") for s in range(1, PARTS)]
 
     new_error = call(
         error_kernel, "error",
@@ -232,15 +250,20 @@
     )
     *own_pieces, new_error = lax.optimization_barrier((*own_pieces, new_error))
     own = jnp.stack(own_pieces)
-    other = along_rep(own, 1)
-    new_base, new_momentum = call(
-        functools.partial(update_kernel, replicas), "update",
-        (own, other, base_params, momentum, col_inv, rows_inv),
-        [VMEM] * 6,
-        [HBM, HBM], [f32(rows, width), f32(rows, width)],
-        [buffer(), buffer(), pltpu.SemaphoreType.DMA((PARTS, 2))],
-        flops=cells * 1024, moved=cells * 16,
-    )
+    other = along_rep(own, 1, "swap")
+    state = ()
+    for half, mean in enumerate((own, other)):
+        piece = pltpu.VMEM((PARTS, rows, width // PARTS // 2), jnp.float32)
+        state = call(
+            functools.partial(update_kernel, replicas, half), "update",
+            (mean, base_params, momentum, col_inv, rows_inv, *state),
+            [VMEM] * 5 + [HBM] * len(state),
+            [HBM, HBM], [f32(rows, width), f32(rows, width)],
+            [piece, piece, pltpu.SemaphoreType.DMA((PARTS, 2))],
+            flops=cells * 512, moved=cells * 8,
+            aliases={5 + i: i for i in range(len(state))},
+        )
+    new_base, new_momentum = state
     return (new_base, new_error, new_momentum)
 
 

time: 51.7 us -> 46.4 us (0.90)
  waiting for transfers between devices: 21.5 us -> 9.59 us
  starting transfers between devices: 18.1 us -> 23.7 us
  Pallas kernels: 9.38 us -> 12.1 us
  local copies, waits for them, and re-layouts: 1.76 us -> 0.05 us
    ppermute x9, waiting for transfers between devices: 17.4 us -> 8.74 us  [along_z(): return lax.ppermute(value, 'fsdp', [(i, i ^ s) for i in range(shards)])]
    ppermute x6, waiting for transfers between devices: 4.15 us -> 0.85 us  [along_rep(): return lax.ppermute(value, 'rep', [(i, i ^ s) for i in range(replicas)])]
    ppermute x9, starting transfers between devices: 10 us -> 12.8 us  [along_z(): return lax.ppermute(value, 'fsdp', [(i, i ^ s) for i in range(shards)])]
    ppermute x6, starting transfers between devices: 8.05 us -> 10.8 us  [along_rep(): return lax.ppermute(value, 'rep', [(i, i ^ s) for i in range(replicas)])]
    pallas_call x3 -> x5, Pallas kernels: 9.38 us -> 12.1 us  [call(): pl.pallas_call(kernel, in_specs=in_specs, out_specs=out_specs, out_shape=...]
    unnamed x12 -> x8, local copies, waits for them, and re-layouts: 1.73 us -> 0.03 us
  transfers between devices with their start and end apart: 15 -> 15, of which waited for: 9 -> 6; matrix products, arithmetic and copies ran while one was open for 0% -> 0% of each run, Pallas kernels for 7% -> 19%
where the time goes in v2:
time: 46.4 us; the launch traced here: 46.3 us
  starting transfers between devices  23.7 us (51%)
  Pallas kernels  12.1 us (26%)
  waiting for transfers between devices  9.59 us (21%)
  between operations  0.77 us (2%)
    ppermute x9, starting transfers between devices, along_z(): return lax.ppermute(value, 'fsdp', [(i, i ^ s) for i in range(shards)])  12.8 us
    pallas_call x5, Pallas kernels, call(): pl.pallas_call(kernel, in_specs=in_specs, out_specs=out_specs, out_shape=...  12.1 us
    ppermute x6, starting transfers between devices, along_rep(): return lax.ppermute(value, 'rep', [(i, i ^ s) for i in range(replicas)])  10.8 us
    ppermute x9, waiting for transfers between devices, along_z(): return lax.ppermute(value, 'fsdp', [(i, i ^ s) for i in range(shards)])  8.74 us
  transfers between devices with their start and end apart: 15, of which 6 were waited for; matrix products, arithmetic and copies ran while one was open for 0% of the time, Pallas kernels for 19%

profile of v2, /device:TPU:1, one launch (start us, length us, event | category | flops | bytes accessed | tf_op | source)
XLA Modules:
  0.0 46.3 jit_solution(1163744070059446091)
XLA Ops:
  0.6 1.8 %forward.3 = f32[1,2,112,128]{3,2,1,0:T(8,128)S(1)} custom-call(f32[16,28672]{1,0:T(8,128)} %base.9, bf16[1,16,28672]{2,1,0:T(8,128)(2,1)} %local.5, f32[1,16,28672]{2,1,0:T(8,128)} %err.5, bf16[512,256]{1,0:T(8,128)(2,1)} %constant.8.clone.col, f32[4,16,16]{2,1,0:T(8,128)} %constant.10.clone.rows), custom_call_target="tpu_custom_call" | custom-call | flops 117440512 | bytes 1261568 | tf_op jit(solution)/shard_map/forward/pallas_call | solution.py:180
  2.4 0.0 copy-start.3
  2.4 3.9 %collective-permute-start.2 = (f32[2,112,128]{2,1,0:T(8,128)S(1)}, f32[2,112,128]{2,1,0:T(8,128)S(1)}, u32[]{:S(2)}, u32[]{:S(2)}) collective-permute-start(f32[2,112,128]{2,1,0:T(8,128)S(1)} %bitcast.23), channel_id=1, source_target_pairs={{0,2},{1,3},{2,0},{3,1},{4,6},{5,7},{6,4},{7,5},{8,10},{9,11},{10,... | collective-permute-start | bytes 344072 | tf_op jit(solution)/shard_map/far2/ppermute | solution.py:223
  6.3 3.3 %forward.2 = f32[3,2,112,128]{3,2,1,0:T(8,128)S(1)} custom-call(f32[16,28672]{1,0:T(8,128)} %base.9, bf16[1,16,28672]{2,1,0:T(8,128)(2,1)} %local.5, f32[1,16,28672]{2,1,0:T(8,128)} %err.5, bf16[512,256]{1,0:T(8,128)(2,1)} %constant.8.clone.col, f32[4,16,16]{2,1,0:T(8,128)} %constant.10.clone.rows), custom_call_target="tpu_custom_call" | custom-call | flops 352321536 | bytes 3784704 | tf_op jit(solution)/shard_map/forward/pallas_call | solution.py:180
  9.6 0.0 copy-start.2
  9.6 1.7 %collective-permute-start = (f32[2,112,128]{2,1,0:T(8,128)S(1)}, f32[2,112,128]{2,1,0:T(8,128)S(1)}, u32[]{:S(2)}, u32[]{:S(2)}) collective-permute-start(f32[2,112,128]{2,1,0:T(8,128)S(1)} %get-tuple-element.29), channel_id=1, source_target_pairs={{0,1},{1,0},{2,3},{3,2},{4,5},{5,4},{6,7},{7,6},{8,9},{9,8},{10,11... | collective-permute-start | bytes 344072 | tf_op jit(solution)/shard_map/near1/ppermute | solution.py:223
  11.4 2.2 %collective-permute-done = f32[2,112,128]{2,1,0:T(8,128)S(1)} collective-permute-done((f32[2,112,128]{2,1,0:T(8,128)S(1)}, f32[2,112,128]{2,1,0:T(8,128)S(1)}, u32[]{:S(2)}, u32[]{:S(2)}) %collective-permute-start) | collective-permute-done | bytes 114720 | tf_op jit(solution)/shard_map/near1/ppermute | solution.py:223
  13.5 3.4 %collective-permute-done.1 = f32[2,112,128]{2,1,0:T(8,128)S(1)} collective-permute-done((f32[2,112,128]{2,1,0:T(8,128)S(1)}, f32[2,112,128]{2,1,0:T(8,128)S(1)}, u32[]{:S(2)}, u32[]{:S(2)}) %collective-permute-start.1) | collective-permute-done | bytes 114720 | tf_op jit(solution)/shard_map/far3/ppermute | solution.py:223
  17.0 2.4 %collective-permute-start.3 = (f32[112,128]{1,0:T(8,128)S(1)}, f32[112,128]{1,0:T(8,128)S(1)}, u32[]{:S(2)}, u32[]{:S(2)}) collective-permute-start(f32[112,128]{1,0:T(8,128)S(1)} %slice_bitcast_fusion.3), channel_id=1, source_target_pairs={{0,16},{16,0},{32,48},{48,32},{64,80},{80,64},{96,112},{112,96},{1... | collective-permute-start | bytes 172040 | tf_op jit(solution)/shard_map/core1/ppermute | solution.py:227
  19.4 1.9 %collective-permute-start.7 = (f32[2,112,128]{2,1,0:T(8,128)S(1)}, f32[2,112,128]{2,1,0:T(8,128)S(1)}, u32[]{:S(2)}, u32[]{:S(2)}) collective-permute-start(f32[2,112,128]{2,1,0:T(8,128)S(1)} %fusion.2.k0), channel_id=1, source_target_pairs={{0,3},{1,2},{2,1},{3,0},{4,7},{5,6},{6,5},{7,4},{8,11},{9,10},{10,... | collective-permute-start | bytes 344072 | tf_op jit(solution)/shard_map/next3/ppermute | solution.py:223
  21.3 0.0 collective-permute-done.3
  21.3 1.4 %collective-permute-start.4 = (f32[112,128]{1,0:T(8,128)S(1)}, f32[112,128]{1,0:T(8,128)S(1)}, u32[]{:S(2)}, u32[]{:S(2)}) collective-permute-start(f32[112,128]{1,0:T(8,128)S(1)} %fusion.3), channel_id=1, source_target_pairs={{0,32},{16,48},{32,0},{48,16},{64,96},{80,112},{96,64},{112,80},{1... | collective-permute-start | bytes 172040 | tf_op jit(solution)/shard_map/ylo2/ppermute | solution.py:227
  22.7 0.0 collective-permute-start.6
  22.7 1.6 %collective-permute-start.5 = (f32[2,112,128]{2,1,0:T(8,128)S(1)}, f32[2,112,128]{2,1,0:T(8,128)S(1)}, u32[]{:S(2)}, u32[]{:S(2)}) collective-permute-start(f32[2,112,128]{2,1,0:T(8,128)S(1)} %fusion.2.k0), channel_id=1, source_target_pairs={{0,1},{1,0},{2,3},{3,2},{4,5},{5,4},{6,7},{7,6},{8,9},{9,8},{10,11... | collective-permute-start | bytes 344072 | tf_op jit(solution)/shard_map/next1/ppermute | solution.py:223
  24.3 0.4 collective-permute-done.4
  24.8 2.8 %collective-permute-start.8 = (f32[112,128]{1,0:T(8,128)S(1)}, f32[112,128]{1,0:T(8,128)S(1)}, u32[]{:S(2)}, u32[]{:S(2)}) collective-permute-start(f32[112,128]{1,0:T(8,128)S(1)} %add.28), channel_id=1, source_target_pairs={{0,128},{16,144},{32,160},{48,176},{64,192},{80,208},{96,224},{112... | collective-permute-start | bytes 172040 | tf_op jit(solution)/shard_map/x8/ppermute | solution.py:227
  27.6 0.9 %collective-permute-start.10 = (f32[112,128]{1,0:T(8,128)S(1)}, f32[112,128]{1,0:T(8,128)S(1)}, u32[]{:S(2)}, u32[]{:S(2)}) collective-permute-start(f32[112,128]{1,0:T(8,128)S(1)} %add.28), channel_id=1, source_target_pairs={{0,192},{16,208},{32,224},{48,240},{64,128},{80,144},{96,160},{112... | collective-permute-start | bytes 172040 | tf_op jit(solution)/shard_map/x12/ppermute | solution.py:227
  28.5 3.1 %collective-permute-done.6.k2 = f32[2,112,128]{2,1,0:T(8,128)S(1)} collective-permute-done((f32[2,112,128]{2,1,0:T(8,128)S(1)}, f32[2,112,128]{2,1,0:T(8,128)S(1)}, u32[]{:S(2)}, u32[]{:S(2)}) %collective-permute-start.6) | collective-permute-done | bytes 114720 | tf_op jit(solution)/shard_map/next2/ppermute | solution.py:223
  31.6 0.0 collective-permute-done.5.k1
  31.6 0.0 collective-permute-done.8
  31.6 0.4 collective-permute-done.10
  32.0 0.1 collective-permute-done.9
  32.1 0.0 copy-start
  32.1 0.0 copy-start.1
  32.1 1.4 %collective-permute-start.13 = (f32[112,128]{1,0:T(8,128)S(1)}, f32[112,128]{1,0:T(8,128)S(1)}, u32[]{:S(2)}, u32[]{:S(2)}) collective-permute-start(f32[112,128]{1,0:T(8,128)S(1)} %add_add_fusion), channel_id=1, source_target_pairs={{0,3},{1,2},{2,1},{3,0},{4,7},{5,6},{6,5},{7,4},{8,11},{9,10},{10,... | collective-permute-start | bytes 172040 | tf_op jit(solution)/shard_map/mean3/ppermute | solution.py:223
  33.5 0.1 collective-permute-start.12
  33.6 2.1 %collective-permute-start.11 = (f32[112,128]{1,0:T(8,128)S(1)}, f32[112,128]{1,0:T(8,128)S(1)}, u32[]{:S(2)}, u32[]{:S(2)}) collective-permute-start(f32[112,128]{1,0:T(8,128)S(1)} %add_add_fusion), channel_id=1, source_target_pairs={{0,1},{1,0},{2,3},{3,2},{4,5},{5,4},{6,7},{7,6},{8,9},{9,8},{10,11... | collective-permute-start | bytes 172040 | tf_op jit(solution)/shard_map/mean1/ppermute | solution.py:223
  35.7 3.6 %error.1 = f32[1,16,28672]{2,1,0:T(8,128)} custom-call(f32[2,112,128]{2,1,0:T(8,128)S(1)} %fusion.2.k0, f32[2,112,128]{2,1,0:T(8,128)S(1)} %collective-permute-done.5.k1, f32[2,112,128]{2,1,0:T(8,128)S(1)} %collective-permute-done.6.k2, f32[2,112,128]{2,1,0:T(8,128)S(1)} %collective-permute-done.7.k3, f32[16,28672]{1,0:T(8,128)} %base.9, ...), custom_call_target="tpu_custom_call" | custom-call | flops 469762048 | bytes 6881280 | tf_op jit(solution)/shard_map/error/pallas_call | solution.py:180
  39.3 0.0 collective-permute-done.13
  39.4 3.4 %collective-permute-start.14 = (f32[4,112,128]{2,1,0:T(8,128)S(1)}, f32[4,112,128]{2,1,0:T(8,128)S(1)}, u32[]{:S(2)}, u32[]{:S(2)}) collective-permute-start(f32[4,112,128]{2,1,0:T(8,128)S(1)} %pad_maximum_fusion.mean), channel_id=1, source_target_pairs={{0,16},{16,0},{32,48},{48,32},{64,80},{80,64},{96,112},{112,96},{1... | collective-permute-start | bytes 688136 | tf_op jit(solution)/shard_map/swap1/ppermute | solution.py:227
  42.8 1.7 %update.2 = (f32[16,28672]{1,0:T(8,128)}, f32[16,28672]{1,0:T(8,128)}) custom-call(f32[4,112,128]{2,1,0:T(8,128)S(1)} %pad_maximum_fusion.mean, f32[16,28672]{1,0:T(8,128)S(1)} %copy-done, f32[16,28672]{1,0:T(8,128)S(1)} %copy-done.1, bf16[2,256,512]{2,1,0:T(8,128)(2,1)S(1)} %copy-done.2, f32[4,16,16]{2,1,0:T(8,128)S(1)} %copy-done.3), custom_call_target="tpu_custom_call" | custom-call | flops 234881024 | bytes 3670016 | tf_op jit(solution)/shard_map/update/pallas_call | solution.py:180
  44.5 1.7 %update.3 = (f32[16,28672]{1,0:T(8,128)}, f32[16,28672]{1,0:T(8,128)}) custom-call(f32[4,112,128]{2,1,0:T(8,128)S(1)} %collective-permute-done.14.mean, f32[16,28672]{1,0:T(8,128)S(1)} %copy-done, f32[16,28672]{1,0:T(8,128)S(1)} %copy-done.1, bf16[2,256,512]{2,1,0:T(8,128)(2,1)S(1)} %copy-done.2, ...), custom_call_target="tpu_custom_call", output_to_operand_aliasing={{0}: (5, {}), {1}: (6, {})} | custom-call | flops 234881024 | bytes 3670016 | tf_op jit(solution)/shard_map/update/pallas_call | solution.py:180
  (18 shorter events, 0.1 us)
Async XLA Ops:
  2.4 33.3 %copy-start.3 = (f32[4,16,16]{2,1,0:T(8,128)S(1)}, f32[4,16,16]{2,1,0:T(8,128)}, u32[]{:S(2)}) copy-start(f32[4,16,16]{2,1,0:T(8,128)} %constant.11.clone.rows) | copy-start | bytes 12292
  2.4 8.9 %collective-permute-start.2 = (f32[2,112,128]{2,1,0:T(8,128)S(1)}, f32[2,112,128]{2,1,0:T(8,128)S(1)}, u32[]{:S(2)}, u32[]{:S(2)}) collective-permute-start(f32[2,112,128]{2,1,0:T(8,128)S(1)} %bitcast.23), channel_id=1, source_target_pairs={{0,2},{1,3},{2,0},{3,1},{4,6},{5,7},{6,4},{7,5},{8,10},{9,11},{10,... | collective-permute-start | bytes 344072 | tf_op jit(solution)/shard_map/far2/ppermute | solution.py:223
  9.6 26.1 %copy-start.2 = (bf16[2,256,512]{2,1,0:T(8,128)(2,1)S(1)}, bf16[2,256,512]{2,1,0:T(8,128)(2,1)}, u32[]{:S(2)}) copy-start(bf16[2,256,512]{2,1,0:T(8,128)(2,1)} %constant.9.clone.col) | copy-start | bytes 1572868
  9.6 3.9 %collective-permute-start = (f32[2,112,128]{2,1,0:T(8,128)S(1)}, f32[2,112,128]{2,1,0:T(8,128)S(1)}, u32[]{:S(2)}, u32[]{:S(2)}) collective-permute-start(f32[2,112,128]{2,1,0:T(8,128)S(1)} %get-tuple-element.29), channel_id=1, source_target_pairs={{0,1},{1,0},{2,3},{3,2},{4,5},{5,4},{6,7},{7,6},{8,9},{9,8},{10,11... | collective-permute-start | bytes 344072 | tf_op jit(solution)/shard_map/near1/ppermute | solution.py:223
  11.4 5.6 %collective-permute-start.1 = (f32[2,112,128]{2,1,0:T(8,128)S(1)}, f32[2,112,128]{2,1,0:T(8,128)S(1)}, u32[]{:S(2)}, u32[]{:S(2)}) collective-permute-start(f32[2,112,128]{2,1,0:T(8,128)S(1)} %get-tuple-element.30), channel_id=1, source_target_pairs={{0,3},{1,2},{2,1},{3,0},{4,7},{5,6},{6,5},{7,4},{8,11},{9,10},{10,... | collective-permute-start | bytes 344072 | tf_op jit(solution)/shard_map/far3/ppermute | solution.py:223
  17.0 4.3 %collective-permute-start.3 = (f32[112,128]{1,0:T(8,128)S(1)}, f32[112,128]{1,0:T(8,128)S(1)}, u32[]{:S(2)}, u32[]{:S(2)}) collective-permute-start(f32[112,128]{1,0:T(8,128)S(1)} %slice_bitcast_fusion.3), channel_id=1, source_target_pairs={{0,16},{16,0},{32,48},{48,32},{64,80},{80,64},{96,112},{112,96},{1... | collective-permute-start | bytes 172040 | tf_op jit(solution)/shard_map/core1/ppermute | solution.py:227
  19.4 9.1 %collective-permute-start.7 = (f32[2,112,128]{2,1,0:T(8,128)S(1)}, f32[2,112,128]{2,1,0:T(8,128)S(1)}, u32[]{:S(2)}, u32[]{:S(2)}) collective-permute-start(f32[2,112,128]{2,1,0:T(8,128)S(1)} %fusion.2.k0), channel_id=1, source_target_pairs={{0,3},{1,2},{2,1},{3,0},{4,7},{5,6},{6,5},{7,4},{8,11},{9,10},{10,... | collective-permute-start | bytes 344072 | tf_op jit(solution)/shard_map/next3/ppermute | solution.py:223
  21.3 3.4 %collective-permute-start.4 = (f32[112,128]{1,0:T(8,128)S(1)}, f32[112,128]{1,0:T(8,128)S(1)}, u32[]{:S(2)}, u32[]{:S(2)}) collective-permute-start(f32[112,128]{1,0:T(8,128)S(1)} %fusion.3), channel_id=1, source_target_pairs={{0,32},{16,48},{32,0},{48,16},{64,96},{80,112},{96,64},{112,80},{1... | collective-permute-start | bytes 172040 | tf_op jit(solution)/shard_map/ylo2/ppermute | solution.py:227
  22.7 8.9 %collective-permute-start.6 = (f32[2,112,128]{2,1,0:T(8,128)S(1)}, f32[2,112,128]{2,1,0:T(8,128)S(1)}, u32[]{:S(2)}, u32[]{:S(2)}) collective-permute-start(f32[2,112,128]{2,1,0:T(8,128)S(1)} %fusion.2.k0), channel_id=1, source_target_pairs={{0,2},{1,3},{2,0},{3,1},{4,6},{5,7},{6,4},{7,5},{8,10},{9,11},{10,... | collective-permute-start | bytes 344072 | tf_op jit(solution)/shard_map/next2/ppermute | solution.py:223
  22.7 8.9 %collective-permute-start.5 = (f32[2,112,128]{2,1,0:T(8,128)S(1)}, f32[2,112,128]{2,1,0:T(8,128)S(1)}, u32[]{:S(2)}, u32[]{:S(2)}) collective-permute-start(f32[2,112,128]{2,1,0:T(8,128)S(1)} %fusion.2.k0), channel_id=1, source_target_pairs={{0,1},{1,0},{2,3},{3,2},{4,5},{5,4},{6,7},{7,6},{8,9},{9,8},{10,11... | collective-permute-start | bytes 344072 | tf_op jit(solution)/shard_map/next1/ppermute | solution.py:223
  24.8 6.9 %collective-permute-start.8 = (f32[112,128]{1,0:T(8,128)S(1)}, f32[112,128]{1,0:T(8,128)S(1)}, u32[]{:S(2)}, u32[]{:S(2)}) collective-permute-start(f32[112,128]{1,0:T(8,128)S(1)} %add.28), channel_id=1, source_target_pairs={{0,128},{16,144},{32,160},{48,176},{64,192},{80,208},{96,224},{112... | collective-permute-start | bytes 172040 | tf_op jit(solution)/shard_map/x8/ppermute | solution.py:227
  27.6 4.4 %collective-permute-start.10 = (f32[112,128]{1,0:T(8,128)S(1)}, f32[112,128]{1,0:T(8,128)S(1)}, u32[]{:S(2)}, u32[]{:S(2)}) collective-permute-start(f32[112,128]{1,0:T(8,128)S(1)} %add.28), channel_id=1, source_target_pairs={{0,192},{16,208},{32,224},{48,240},{64,128},{80,144},{96,160},{112... | collective-permute-start | bytes 172040 | tf_op jit(solution)/shard_map/x12/ppermute | solution.py:227
  28.5 3.6 %collective-permute-start.9 = (f32[112,128]{1,0:T(8,128)S(1)}, f32[112,128]{1,0:T(8,128)S(1)}, u32[]{:S(2)}, u32[]{:S(2)}) collective-permute-start(f32[112,128]{1,0:T(8,128)S(1)} %add.28), channel_id=1, source_target_pairs={{0,64},{16,80},{32,96},{48,112},{64,0},{80,16},{96,32},{112,48},{1... | collective-permute-start | bytes 172040 | tf_op jit(solution)/shard_map/x4/ppermute | solution.py:227
  32.1 10.7 %copy-start = (f32[16,28672]{1,0:T(8,128)S(1)}, f32[16,28672]{1,0:T(8,128)}, u32[]{:S(2)}) copy-start(f32[16,28672]{1,0:T(8,128)} %base.9) | copy-start | bytes 5505028
  32.1 10.7 %copy-start.1 = (f32[16,28672]{1,0:T(8,128)S(1)}, f32[16,28672]{1,0:T(8,128)}, u32[]{:S(2)}) copy-start(f32[16,28672]{1,0:T(8,128)} %mom.3) | copy-start | bytes 5505028
  32.1 7.2 %collective-permute-start.13 = (f32[112,128]{1,0:T(8,128)S(1)}, f32[112,128]{1,0:T(8,128)S(1)}, u32[]{:S(2)}, u32[]{:S(2)}) collective-permute-start(f32[112,128]{1,0:T(8,128)S(1)} %add_add_fusion), channel_id=1, source_target_pairs={{0,3},{1,2},{2,1},{3,0},{4,7},{5,6},{6,5},{7,4},{8,11},{9,10},{10,... | collective-permute-start | bytes 172040 | tf_op jit(solution)/shard_map/mean3/ppermute | solution.py:223
  33.5 5.9 %collective-permute-start.12 = (f32[112,128]{1,0:T(8,128)S(1)}, f32[112,128]{1,0:T(8,128)S(1)}, u32[]{:S(2)}, u32[]{:S(2)}) collective-permute-start(f32[112,128]{1,0:T(8,128)S(1)} %add_add_fusion), channel_id=1, source_target_pairs={{0,2},{1,3},{2,0},{3,1},{4,6},{5,7},{6,4},{7,5},{8,10},{9,11},{10,... | collective-permute-start | bytes 172040 | tf_op jit(solution)/shard_map/mean2/ppermute | solution.py:223
  33.6 5.8 %collective-permute-start.11 = (f32[112,128]{1,0:T(8,128)S(1)}, f32[112,128]{1,0:T(8,128)S(1)}, u32[]{:S(2)}, u32[]{:S(2)}) collective-permute-start(f32[112,128]{1,0:T(8,128)S(1)} %add_add_fusion), channel_id=1, source_target_pairs={{0,1},{1,0},{2,3},{3,2},{4,5},{5,4},{6,7},{7,6},{8,9},{9,8},{10,11... | collective-permute-start | bytes 172040 | tf_op jit(solution)/shard_map/mean1/ppermute | solution.py:223
  39.4 5.1 %collective-permute-start.14 = (f32[4,112,128]{2,1,0:T(8,128)S(1)}, f32[4,112,128]{2,1,0:T(8,128)S(1)}, u32[]{:S(2)}, u32[]{:S(2)}) collective-permute-start(f32[4,112,128]{2,1,0:T(8,128)S(1)} %pad_maximum_fusion.mean), channel_id=1, source_target_pairs={{0,16},{16,0},{32,48},{48,32},{64,80},{80,64},{96,112},{112,96},{1... | collective-permute-start | bytes 688136 | tf_op jit(solution)/shard_map/swap1/ppermute | solution.py:227

commit v3 on v2

--- a/solution.py
+++ b/solution.py
@@ -20,7 +20,7 @@
 GROUP_TILES = 8
 GROUP = GROUP_TILES * TILE
 WIDE = GROUP_TILES * BAND
-VMEM_LIMIT = 40 * 1024 * 1024
+VMEM_LIMIT = 24 * 1024 * 1024
 
 HBM = pl.BlockSpec(memory_space=pltpu.HBM)
 VMEM = pl.BlockSpec(memory_space=pltpu.VMEM)
@@ -76,7 +76,7 @@
     return pl.ds(pl.multiple_of((part ^ s) * size, GROUP), size)
 
 
-def forward_kernel(steps, base, local, err, col, rows, out, base_v, local_v, err_v, col_v, rows_v, sems, table_sems):
+def forward_kernel(steps, base, local, err, col, rows, out, kept, base_v, local_v, err_v, col_v, rows_v, sems, table_sems):
     part, core = position()
     width = base.shape[1]
     tables = (
@@ -95,22 +95,24 @@
         )
     for copy in (*copies[0], *tables, *(copy for step in copies[1:] for copy in step)):
         copy.start()
+    for copy in (*tables, *(copy for step in copies for copy in step)):
+        copy.wait()
+    stacked = []
     for i in range(len(steps)):
-        for copy in copies[i]:
-            copy.wait()
-        if i == 0:
-            for copy in tables:
-                copy.wait()
-        field = base_v[i] - local_v[i].astype(jnp.float32) + err_v[i]
-        groups = field.shape[1] // GROUP
-        stacked = jnp.concatenate([field[:, GROUP * g : GROUP * (g + 1)] for g in range(groups)], axis=0)
-        count = stacked.shape[0]
-        both = dot(jnp.concatenate(split(stacked), axis=0), col_v[...])
-        both = both[:, :WIDE] + both[:, WIDE:]
-        coeffs = apply_rows(rows_v[...], both[:count] + both[count:])
-        half = count // 2
-        out[i, core] = coeffs[:half]
-        out[i, 1 - core] = coeffs[half:]
+        for g in range(base_v.shape[2] // GROUP):
+            at = slice(GROUP * g, GROUP * (g + 1))
+            field = base_v[i, :, at] - local_v[i, :, at].astype(jnp.float32) + err_v[i, :, at]
+            kept[i, :, at] = field
+            stacked.append(field)
+    stacked = jnp.concatenate(stacked, axis=0)
+    count = stacked.shape[0]
+    both = dot(jnp.concatenate(split(stacked), axis=0), col_v[...])
+    both = both[:, :WIDE] + both[:, WIDE:]
+    coeffs = apply_rows(rows_v[...], both[:count] + both[count:])
+    half = count // len(steps) // 2
+    for i in range(len(steps)):
+        out[i, core] = coeffs[2 * i * half : (2 * i + 1) * half]
+        out[i, 1 - core] = coeffs[(2 * i + 1) * half : (2 * i + 2) * half]
 
 
 def inverse_rows(table, col, coeffs):
@@ -118,59 +120,45 @@
     return dot(both, col[0]) + dot(both, col[1])
 
 
-def error_kernel(k0, k1, k2, k3, base, local, err, col, rows, out, base_v, local_v, err_v, out_v, sems):
+def error_kernel(k0, k1, k2, k3, field3, fields, col, rows, out, out_v, sems):
     part, core = position()
-    width = base.shape[1]
-    copies, writes = [], []
-    for s in range(PARTS):
-        cols = quarter_cols(part, s, width)
-        copies.append(
-            [
-                pltpu.make_async_copy(base.at[:, cols], base_v.at[s], sems.at[s, 0]),
-                pltpu.make_async_copy(err.at[0, :, cols], err_v.at[s], sems.at[s, 1]),
-                pltpu.make_async_copy(local.at[0, :, cols], local_v.at[s], sems.at[s, 2]),
-            ]
-        )
-        writes.append(pltpu.make_async_copy(out_v.at[s], out.at[0, :, cols], sems.at[s, 3]))
-    for step in copies:
-        for copy in step:
-            copy.start()
-    table = rows[part]
-    for s, k in enumerate((k0, k1, k2, k3)):
-        coeffs = jnp.concatenate([k[core], k[1 - core]], axis=0)
-        kept = inverse_rows(table, col, coeffs)
-        for copy in copies[s]:
-            copy.wait()
-        for g in range(coeffs.shape[0] // ROWS):
+    width = out.shape[2]
+    order = ((k0, fields.at[2]), (k1, fields.at[1]), (k2, fields.at[0]), (k3, field3.at[0]))
+    coeffs = jnp.concatenate([k[h] for k, _ in order for h in (core, 1 - core)], axis=0)
+    kept = inverse_rows(rows[part], col, coeffs)
+    count = coeffs.shape[0] // PARTS
+    writes = []
+    for s, (_, field) in enumerate(order):
+        for g in range(count // ROWS):
+            row = s * count + ROWS * g
             at = slice(GROUP * g, GROUP * (g + 1))
-            field = base_v[s, :, at] - local_v[s, :, at].astype(jnp.float32) + err_v[s, :, at]
-            out_v[s, :, at] = field - kept[ROWS * g : ROWS * (g + 1)]
-        writes[s].start()
+            out_v[s, :, at] = field[:, at] - kept[row : row + ROWS]
+        writes.append(pltpu.make_async_copy(out_v.at[s], out.at[0, :, quarter_cols(part, s, width)], sems.at[s]))
+        writes[-1].start()
     for write in writes:
         write.wait()
 
 
-def update_kernel(replicas, half, mean, base, mom, col, rows, *refs):
+def update_kernel(replicas, pieces, base, mom, col, rows, *refs):
     base_out, mom_out, base_w, mom_w, sems = refs[-5:]
     part, core = position()
     width = base.shape[1]
+    size = width // PARTS // 2
     table = rows[part]
-    size = width // PARTS // 2
-    here = core if half == 0 else 1 - core
     writes = []
-    for s in range(PARTS):
-        start = ((part ^ s) * 2 + here) * size
-        outer = inverse_rows(table, col, mean[s] * (1.0 / replicas))
+    for n, (s, half, which, index) in enumerate(pieces):
+        outer = inverse_rows(table, col, refs[which][index] * (1.0 / replicas))
+        start = ((part ^ s) * 2 + (core if half == 0 else 1 - core)) * size
         for g in range(size // GROUP):
             at = slice(GROUP * g, GROUP * (g + 1))
             src = pl.ds(pl.multiple_of(start + GROUP * g, GROUP), GROUP)
             grad = outer[ROWS * g : ROWS * (g + 1)]
             new_momentum = OUTER_BETA * mom[:, src] + grad
-            mom_w[s, :, at] = new_momentum
-            base_w[s, :, at] = base[:, src] - OUTER_RATE * (grad + OUTER_BETA * new_momentum)
+            mom_w[n, :, at] = new_momentum
+            base_w[n, :, at] = base[:, src] - OUTER_RATE * (grad + OUTER_BETA * new_momentum)
         cols = pl.ds(pl.multiple_of(start, GROUP), size)
         for i, (src, dst) in enumerate(((base_w, base_out), (mom_w, mom_out))):
-            writes.append(pltpu.make_async_copy(src.at[s], dst.at[:, cols], sems.at[s, i]))
+            writes.append(pltpu.make_async_copy(src.at[n], dst.at[:, cols], sems.at[n, i]))
             writes[-1].start()
     for write in writes:
         write.wait()
@@ -207,16 +195,16 @@
     def forward(*steps):
         count = len(steps)
         pair = lambda dtype=jnp.float32: pltpu.VMEM((count, rows, width // PARTS), dtype)
-        coeffs = call(
+        coeffs, field = call(
             functools.partial(forward_kernel, steps), "forward",
             [in_hbm(v) for v in (base_params, local_params, error_buffer, col_fwd, rows_fwd)],
             [HBM] * 5,
-            VMEM, pltpu.VMEM((count, 2, quarter_rows // 2, WIDE), jnp.float32),
+            [VMEM, VMEM], [pltpu.VMEM((count, 2, quarter_rows // 2, WIDE), jnp.float32), pair()],
             [pair(), pair(jnp.bfloat16), pair(), pltpu.VMEM(col_fwd.shape, jnp.bfloat16), pltpu.VMEM(rows_fwd.shape[1:], jnp.float32),
              pltpu.SemaphoreType.DMA((count, 3)), pltpu.SemaphoreType.DMA((2,))],
             flops=cells * 256 * count, moved=cells * 11 * count // PARTS,
         )
-        return tuple(coeffs[i] for i in range(count))
+        return tuple(coeffs[i] for i in range(count)), field
 
     def along_z(value, s, name):
         with jax.named_scope(f"{name}{s}"):
@@ -226,12 +214,13 @@
         with jax.named_scope(f"{name}{s}"):
             return lax.ppermute(value, "rep", [(i, i ^ s) for i in range(replicas)])
 
-    (part2,) = forward(2)
-    far2 = along_z(part2, 2, "far")
-    part3, part1, part0 = forward(3, 1, 0)
+    (part3,), field3 = forward(3)
+    passed = along_z(part3, 1, "pass")
+    (part2, part1, part0), fields = forward(2, 1, 0)
+    passed, part1 = lax.optimization_barrier((passed, part1))
+    far2 = along_z(part2 + passed, 2, "far")
     near1 = along_z(part1, 1, "near")
-    far3 = along_z(part3, 3, "far")
-    quarter = part0 + near1 + far3 + far2
+    quarter = part0 + far2 + near1
     total = quarter[0] + along_rep(quarter[1], 1, "core")
     total = total + along_rep(total, 2, "ylo")
     x12, x4, x8 = (along_rep(total, s, "x") for s in (12, 4, 8))
@@ -242,26 +231,31 @@
 
     new_error = call(
         error_kernel, "error",
-        (quarter, next1, next2, next3, in_hbm(base_params), in_hbm(local_params), in_hbm(error_buffer), col_inv, rows_inv),
-        [VMEM] * PARTS + [HBM, HBM, HBM, VMEM, VMEM],
+        (quarter, next1, next2, next3, field3, fields, col_inv, rows_inv),
+        [VMEM] * 8,
         HBM, f32(1, rows, width),
-        [buffer(), buffer(jnp.bfloat16), buffer(), buffer(), pltpu.SemaphoreType.DMA((PARTS, 4))],
-        flops=cells * 1024, moved=cells * 15,
+        [buffer(), pltpu.SemaphoreType.DMA((PARTS,))],
+        flops=cells * 1024, moved=cells * 8,
     )
     *own_pieces, new_error = lax.optimization_barrier((*own_pieces, new_error))
     own = jnp.stack(own_pieces)
     other = along_rep(own, 1, "swap")
+    batches = (
+        ((own,), tuple((s, 0, 0, s) for s in range(PARTS))),
+        ((other,), tuple((s, 1, 0, s) for s in range(PARTS))),
+    )
     state = ()
-    for half, mean in enumerate((own, other)):
-        piece = pltpu.VMEM((PARTS, rows, width // PARTS // 2), jnp.float32)
+    for means, pieces in batches:
+        count = len(pieces)
+        piece = pltpu.VMEM((count, rows, width // PARTS // 2), jnp.float32)
         state = call(
-            functools.partial(update_kernel, replicas, half), "update",
-            (mean, base_params, momentum, col_inv, rows_inv, *state),
-            [VMEM] * 5 + [HBM] * len(state),
+            functools.partial(update_kernel, replicas, pieces), "update",
+            (base_params, momentum, col_inv, rows_inv, *means, *state),
+            [VMEM] * (4 + len(means)) + [HBM] * len(state),
             [HBM, HBM], [f32(rows, width), f32(rows, width)],
-            [piece, piece, pltpu.SemaphoreType.DMA((PARTS, 2))],
-            flops=cells * 512, moved=cells * 8,
-            aliases={5 + i: i for i in range(len(state))},
+            [piece, piece, pltpu.SemaphoreType.DMA((count, 2))],
+            flops=cells * 128 * count, moved=cells * 2 * count,
+            aliases={4 + len(means) + i: i for i in range(len(state))},
         )
     new_base, new_momentum = state
     return (new_base, new_error, new_momentum)

time: 46.4 us -> 45 us (0.970)
  Pallas kernels: 12.1 us -> 10.2 us
    pallas_call x5, Pallas kernels: 12.1 us -> 10.2 us  [call(): pl.pallas_call(kernel, in_specs=in_specs, out_specs=out_specs, out_shape=...]
    ppermute x9, starting transfers between devices: 12.8 us -> 13.8 us  [along_z(): return lax.ppermute(value, 'fsdp', [(i, i ^ s) for i in range(shards)])]
    ppermute x6, starting transfers between devices: 10.8 us -> 10.1 us  [along_rep(): return lax.ppermute(value, 'rep', [(i, i ^ s) for i in range(replicas)])]
    ppermute x6, waiting for transfers between devices: 0.85 us -> 1.36 us  [along_rep(): return lax.ppermute(value, 'rep', [(i, i ^ s) for i in range(replicas)])]
  transfers between devices with their start and end apart: 15 -> 15, of which waited for: 6 -> 6; matrix products, arithmetic and copies ran while one was open for 0% -> 0% of each run, Pallas kernels for 19% -> 15%
where the time goes in v3:
time: 45 us; the launch traced here: 44.9 us
  starting transfers between devices  24 us (53%)
  Pallas kernels  10.2 us (23%)
  waiting for transfers between devices  9.82 us (22%)
  between operations  0.76 us (2%)
    ppermute x9, starting transfers between devices, along_z(): return lax.ppermute(value, 'fsdp', [(i, i ^ s) for i in range(shards)])  13.8 us
    pallas_call x5, Pallas kernels, call(): pl.pallas_call(kernel, in_specs=in_specs, out_specs=out_specs, out_shape=...  10.2 us
    ppermute x6, starting transfers between devices, along_rep(): return lax.ppermute(value, 'rep', [(i, i ^ s) for i in range(replicas)])  10.1 us
    ppermute x9, waiting for transfers between devices, along_z(): return lax.ppermute(value, 'fsdp', [(i, i ^ s) for i in range(shards)])  8.46 us
    ppermute x6, waiting for transfers between devices, along_rep(): return lax.ppermute(value, 'rep', [(i, i ^ s) for i in range(replicas)])  1.36 us
  transfers between devices with their start and end apart: 15, of which 6 were waited for; matrix products, arithmetic and copies ran while one was open for 0% of the time, Pallas kernels for 15%

profile of v3, /device:TPU:1, one launch (start us, length us, event | category | flops | bytes accessed | tf_op | source)
XLA Modules:
  0.0 44.9 jit_solution(16233980215331978964)
XLA Ops:
  0.6 1.8 %forward.3 = (f32[1,2,112,128]{3,2,1,0:T(8,128)S(1)}, f32[1,16,7168]{2,1,0:T(8,128)S(1)}) custom-call(f32[16,28672]{1,0:T(8,128)} %base.7, bf16[1,16,28672]{2,1,0:T(8,128)(2,1)} %local.3, f32[1,16,28672]{2,1,0:T(8,128)} %err.3, bf16[512,256]{1,0:T(8,128)(2,1)} %constant.8.clone.col, f32[4,16,16]{2,1,0:T(8,128)} %constant.10.clone.rows), custom_call_target="tpu_custom_call" | custom-call | flops 117440512 | bytes 1261568 | tf_op jit(solution)/shard_map/forward/pallas_call | solution.py:168
  2.4 0.0 copy-start.3
  2.4 2.6 %collective-permute-start = (f32[2,112,128]{2,1,0:T(8,128)S(1)}, f32[2,112,128]{2,1,0:T(8,128)S(1)}, u32[]{:S(2)}, u32[]{:S(2)}) collective-permute-start(f32[2,112,128]{2,1,0:T(8,128)S(1)} %bitcast.19), channel_id=1, source_target_pairs={{0,1},{1,0},{2,3},{3,2},{4,5},{5,4},{6,7},{7,6},{8,9},{9,8},{10,11... | collective-permute-start | bytes 344072 | tf_op jit(solution)/shard_map/pass1/ppermute | solution.py:211
  5.0 3.0 %forward.2 = (f32[3,2,112,128]{3,2,1,0:T(8,128)S(1)}, f32[3,16,7168]{2,1,0:T(8,128)S(1)}) custom-call(f32[16,28672]{1,0:T(8,128)} %base.7, bf16[1,16,28672]{2,1,0:T(8,128)(2,1)} %local.3, f32[1,16,28672]{2,1,0:T(8,128)} %err.3, bf16[512,256]{1,0:T(8,128)(2,1)} %constant.8.clone.col, f32[4,16,16]{2,1,0:T(8,128)} %constant.10.clone.rows), custom_call_target="tpu_custom_call" | custom-call | flops 352321536 | bytes 3784704 | tf_op jit(solution)/shard_map/forward/pallas_call | solution.py:168
  7.9 0.0 copy-start.2
  8.0 0.0 collective-permute-done
  8.0 3.1 %collective-permute-start.1 = (f32[2,112,128]{2,1,0:T(8,128)S(1)}, f32[2,112,128]{2,1,0:T(8,128)S(1)}, u32[]{:S(2)}, u32[]{:S(2)}) collective-permute-start(f32[2,112,128]{2,1,0:T(8,128)S(1)} %bitcast_add_fusion), channel_id=1, source_target_pairs={{0,2},{1,3},{2,0},{3,1},{4,6},{5,7},{6,4},{7,5},{8,10},{9,11},{10,... | collective-permute-start | bytes 344072 | tf_op jit(solution)/shard_map/far2/ppermute | solution.py:211
  11.1 1.0 %collective-permute-start.2 = (f32[2,112,128]{2,1,0:T(8,128)S(1)}, f32[2,112,128]{2,1,0:T(8,128)S(1)}, u32[]{:S(2)}, u32[]{:S(2)}) collective-permute-start(f32[2,112,128]{2,1,0:T(8,128)S(1)} %slice_bitcast_fusion), channel_id=1, source_target_pairs={{0,1},{1,0},{2,3},{3,2},{4,5},{5,4},{6,7},{7,6},{8,9},{9,8},{10,11... | collective-permute-start | bytes 344072 | tf_op jit(solution)/shard_map/near1/ppermute | solution.py:211
  12.1 2.7 %collective-permute-done.1 = f32[2,112,128]{2,1,0:T(8,128)S(1)} collective-permute-done((f32[2,112,128]{2,1,0:T(8,128)S(1)}, f32[2,112,128]{2,1,0:T(8,128)S(1)}, u32[]{:S(2)}, u32[]{:S(2)}) %collective-permute-start.1) | collective-permute-done | bytes 114720 | tf_op jit(solution)/shard_map/far2/ppermute | solution.py:211
  14.8 1.7 %collective-permute-done.2 = f32[2,112,128]{2,1,0:T(8,128)S(1)} collective-permute-done((f32[2,112,128]{2,1,0:T(8,128)S(1)}, f32[2,112,128]{2,1,0:T(8,128)S(1)}, u32[]{:S(2)}, u32[]{:S(2)}) %collective-permute-start.2) | collective-permute-done | bytes 114720 | tf_op jit(solution)/shard_map/near1/ppermute | solution.py:211
  16.5 1.9 %collective-permute-start.3 = (f32[112,128]{1,0:T(8,128)S(1)}, f32[112,128]{1,0:T(8,128)S(1)}, u32[]{:S(2)}, u32[]{:S(2)}) collective-permute-start(f32[112,128]{1,0:T(8,128)S(1)} %slice_bitcast_fusion.1), channel_id=1, source_target_pairs={{0,16},{16,0},{32,48},{48,32},{64,80},{80,64},{96,112},{112,96},{1... | collective-permute-start | bytes 172040 | tf_op jit(solution)/shard_map/core1/ppermute | solution.py:215
  18.4 2.4 %collective-permute-start.7 = (f32[2,112,128]{2,1,0:T(8,128)S(1)}, f32[2,112,128]{2,1,0:T(8,128)S(1)}, u32[]{:S(2)}, u32[]{:S(2)}) collective-permute-start(f32[2,112,128]{2,1,0:T(8,128)S(1)} %fusion.k0), channel_id=1, source_target_pairs={{0,3},{1,2},{2,1},{3,0},{4,7},{5,6},{6,5},{7,4},{8,11},{9,10},{10,... | collective-permute-start | bytes 344072 | tf_op jit(solution)/shard_map/next3/ppermute | solution.py:211
  20.8 0.0 collective-permute-done.3
  20.9 1.4 %collective-permute-start.4 = (f32[112,128]{1,0:T(8,128)S(1)}, f32[112,128]{1,0:T(8,128)S(1)}, u32[]{:S(2)}, u32[]{:S(2)}) collective-permute-start(f32[112,128]{1,0:T(8,128)S(1)} %fusion.1), channel_id=1, source_target_pairs={{0,32},{16,48},{32,0},{48,16},{64,96},{80,112},{96,64},{112,80},{1... | collective-permute-start | bytes 172040 | tf_op jit(solution)/shard_map/ylo2/ppermute | solution.py:215
  22.2 0.0 collective-permute-start.6
  22.2 1.1 %collective-permute-start.5 = (f32[2,112,128]{2,1,0:T(8,128)S(1)}, f32[2,112,128]{2,1,0:T(8,128)S(1)}, u32[]{:S(2)}, u32[]{:S(2)}) collective-permute-start(f32[2,112,128]{2,1,0:T(8,128)S(1)} %fusion.k0), channel_id=1, source_target_pairs={{0,1},{1,0},{2,3},{3,2},{4,5},{5,4},{6,7},{7,6},{8,9},{9,8},{10,11... | collective-permute-start | bytes 344072 | tf_op jit(solution)/shard_map/next1/ppermute | solution.py:211
  23.4 0.9 %collective-permute-done.4 = f32[112,128]{1,0:T(8,128)S(1)} collective-permute-done((f32[112,128]{1,0:T(8,128)S(1)}, f32[112,128]{1,0:T(8,128)S(1)}, u32[]{:S(2)}, u32[]{:S(2)}) %collective-permute-start.4) | collective-permute-done | bytes 57376 | tf_op jit(solution)/shard_map/ylo2/ppermute | solution.py:215
  24.3 2.8 %collective-permute-start.8 = (f32[112,128]{1,0:T(8,128)S(1)}, f32[112,128]{1,0:T(8,128)S(1)}, u32[]{:S(2)}, u32[]{:S(2)}) collective-permute-start(f32[112,128]{1,0:T(8,128)S(1)} %add.28), channel_id=1, source_target_pairs={{0,128},{16,144},{32,160},{48,176},{64,192},{80,208},{96,224},{112... | collective-permute-start | bytes 172040 | tf_op jit(solution)/shard_map/x8/ppermute | solution.py:215
  27.1 0.9 %collective-permute-start.10 = (f32[112,128]{1,0:T(8,128)S(1)}, f32[112,128]{1,0:T(8,128)S(1)}, u32[]{:S(2)}, u32[]{:S(2)}) collective-permute-start(f32[112,128]{1,0:T(8,128)S(1)} %add.28), channel_id=1, source_target_pairs={{0,192},{16,208},{32,224},{48,240},{64,128},{80,144},{96,160},{112... | collective-permute-start | bytes 172040 | tf_op jit(solution)/shard_map/x12/ppermute | solution.py:215
  28.0 3.1 %collective-permute-done.6.k2 = f32[2,112,128]{2,1,0:T(8,128)S(1)} collective-permute-done((f32[2,112,128]{2,1,0:T(8,128)S(1)}, f32[2,112,128]{2,1,0:T(8,128)S(1)}, u32[]{:S(2)}, u32[]{:S(2)}) %collective-permute-start.6) | collective-permute-done | bytes 114720 | tf_op jit(solution)/shard_map/next2/ppermute | solution.py:211
  31.1 0.4 collective-permute-done.10
  31.5 0.0 collective-permute-done.9
  31.6 1.4 %collective-permute-start.13 = (f32[112,128]{1,0:T(8,128)S(1)}, f32[112,128]{1,0:T(8,128)S(1)}, u32[]{:S(2)}, u32[]{:S(2)}) collective-permute-start(f32[112,128]{1,0:T(8,128)S(1)} %add_add_fusion), channel_id=1, source_target_pairs={{0,3},{1,2},{2,1},{3,0},{4,7},{5,6},{6,5},{7,4},{8,11},{9,10},{10,... | collective-permute-start | bytes 172040 | tf_op jit(solution)/shard_map/mean3/ppermute | solution.py:211
  33.0 0.2 collective-permute-start.12
  33.2 2.0 %collective-permute-start.11 = (f32[112,128]{1,0:T(8,128)S(1)}, f32[112,128]{1,0:T(8,128)S(1)}, u32[]{:S(2)}, u32[]{:S(2)}) collective-permute-start(f32[112,128]{1,0:T(8,128)S(1)} %add_add_fusion), channel_id=1, source_target_pairs={{0,1},{1,0},{2,3},{3,2},{4,5},{5,4},{6,7},{7,6},{8,9},{9,8},{10,11... | collective-permute-start | bytes 172040 | tf_op jit(solution)/shard_map/mean1/ppermute | solution.py:211
  35.2 2.1 %error.1 = f32[1,16,28672]{2,1,0:T(8,128)} custom-call(f32[2,112,128]{2,1,0:T(8,128)S(1)} %fusion.k0, f32[2,112,128]{2,1,0:T(8,128)S(1)} %collective-permute-done.5.k1, f32[2,112,128]{2,1,0:T(8,128)S(1)} %collective-permute-done.6.k2, f32[2,112,128]{2,1,0:T(8,128)S(1)} %collective-permute-done.7.k3, f32[1,16,7168]{2,1,0:T(8,128)S(1)} %get-tuple-element.30.field3, ...), custom_call_target="tpu_custom_call" | custom-call | flops 469762048 | bytes 3670016 | tf_op jit(solution)/shard_map/error/pallas_call | solution.py:168
  37.3 0.0 collective-permute-done.13
  37.3 0.9 %collective-permute-done.12 = f32[112,128]{1,0:T(8,128)S(1)} collective-permute-done((f32[112,128]{1,0:T(8,128)S(1)}, f32[112,128]{1,0:T(8,128)S(1)}, u32[]{:S(2)}, u32[]{:S(2)}) %collective-permute-start.12) | collective-permute-done | bytes 57376 | tf_op jit(solution)/shard_map/mean2/ppermute | solution.py:211
  38.2 0.0 collective-permute-done.11
  38.3 3.2 %collective-permute-start.14 = (f32[4,112,128]{2,1,0:T(8,128)S(1)}, f32[4,112,128]{2,1,0:T(8,128)S(1)}, u32[]{:S(2)}, u32[]{:S(2)}) collective-permute-start(f32[4,112,128]{2,1,0:T(8,128)S(1)} %pad_maximum_fusion.refs_0_), channel_id=1, source_target_pairs={{0,16},{16,0},{32,48},{48,32},{64,80},{80,64},{96,112},{112,96},{1... | collective-permute-start | bytes 688136 | tf_op jit(solution)/shard_map/swap1/ppermute | solution.py:215
  41.4 1.7 %update.2 = (f32[16,28672]{1,0:T(8,128)}, f32[16,28672]{1,0:T(8,128)}) custom-call(f32[16,28672]{1,0:T(8,128)S(1)} %copy-done, f32[16,28672]{1,0:T(8,128)S(1)} %copy-done.1, bf16[2,256,512]{2,1,0:T(8,128)(2,1)S(1)} %copy-done.2, f32[4,16,16]{2,1,0:T(8,128)S(1)} %copy-done.3, f32[4,112,128]{2,1,0:T(8,128)S(1)} %pad_maximum_fusion.refs_0_), custom_call_target="tpu_custom_call" | custom-call | flops 234881024 | bytes 3670016 | tf_op jit(solution)/shard_map/update/pallas_call | solution.py:168
  43.2 1.7 %update.3 = (f32[16,28672]{1,0:T(8,128)}, f32[16,28672]{1,0:T(8,128)}) custom-call(f32[16,28672]{1,0:T(8,128)S(1)} %copy-done, f32[16,28672]{1,0:T(8,128)S(1)} %copy-done.1, bf16[2,256,512]{2,1,0:T(8,128)(2,1)S(1)} %copy-done.2, f32[4,16,16]{2,1,0:T(8,128)S(1)} %copy-done.3, ...), custom_call_target="tpu_custom_call", output_to_operand_aliasing={{0}: (5, {}), {1}: (6, {})} | custom-call | flops 234881024 | bytes 3670016 | tf_op jit(solution)/shard_map/update/pallas_call | solution.py:168
  (19 shorter events, 0.1 us)
Async XLA Ops:
  2.4 32.8 %copy-start.3 = (f32[4,16,16]{2,1,0:T(8,128)S(1)}, f32[4,16,16]{2,1,0:T(8,128)}, u32[]{:S(2)}) copy-start(f32[4,16,16]{2,1,0:T(8,128)} %constant.11.clone.rows) | copy-start | bytes 12292
  2.4 5.6 %collective-permute-start = (f32[2,112,128]{2,1,0:T(8,128)S(1)}, f32[2,112,128]{2,1,0:T(8,128)S(1)}, u32[]{:S(2)}, u32[]{:S(2)}) collective-permute-start(f32[2,112,128]{2,1,0:T(8,128)S(1)} %bitcast.19), channel_id=1, source_target_pairs={{0,1},{1,0},{2,3},{3,2},{4,5},{5,4},{6,7},{7,6},{8,9},{9,8},{10,11... | collective-permute-start | bytes 344072 | tf_op jit(solution)/shard_map/pass1/ppermute | solution.py:211
  7.9 27.3 %copy-start.2 = (bf16[2,256,512]{2,1,0:T(8,128)(2,1)S(1)}, bf16[2,256,512]{2,1,0:T(8,128)(2,1)}, u32[]{:S(2)}) copy-start(bf16[2,256,512]{2,1,0:T(8,128)(2,1)} %constant.9.clone.col) | copy-start | bytes 1572868
  8.0 6.8 %collective-permute-start.1 = (f32[2,112,128]{2,1,0:T(8,128)S(1)}, f32[2,112,128]{2,1,0:T(8,128)S(1)}, u32[]{:S(2)}, u32[]{:S(2)}) collective-permute-start(f32[2,112,128]{2,1,0:T(8,128)S(1)} %bitcast_add_fusion), channel_id=1, source_target_pairs={{0,2},{1,3},{2,0},{3,1},{4,6},{5,7},{6,4},{7,5},{8,10},{9,11},{10,... | collective-permute-start | bytes 344072 | tf_op jit(solution)/shard_map/far2/ppermute | solution.py:211
  11.1 5.4 %collective-permute-start.2 = (f32[2,112,128]{2,1,0:T(8,128)S(1)}, f32[2,112,128]{2,1,0:T(8,128)S(1)}, u32[]{:S(2)}, u32[]{:S(2)}) collective-permute-start(f32[2,112,128]{2,1,0:T(8,128)S(1)} %slice_bitcast_fusion), channel_id=1, source_target_pairs={{0,1},{1,0},{2,3},{3,2},{4,5},{5,4},{6,7},{7,6},{8,9},{9,8},{10,11... | collective-permute-start | bytes 344072 | tf_op jit(solution)/shard_map/near1/ppermute | solution.py:211
  16.5 4.3 %collective-permute-start.3 = (f32[112,128]{1,0:T(8,128)S(1)}, f32[112,128]{1,0:T(8,128)S(1)}, u32[]{:S(2)}, u32[]{:S(2)}) collective-permute-start(f32[112,128]{1,0:T(8,128)S(1)} %slice_bitcast_fusion.1), channel_id=1, source_target_pairs={{0,16},{16,0},{32,48},{48,32},{64,80},{80,64},{96,112},{112,96},{1... | collective-permute-start | bytes 172040 | tf_op jit(solution)/shard_map/core1/ppermute | solution.py:215
  18.4 9.6 %collective-permute-start.7 = (f32[2,112,128]{2,1,0:T(8,128)S(1)}, f32[2,112,128]{2,1,0:T(8,128)S(1)}, u32[]{:S(2)}, u32[]{:S(2)}) collective-permute-start(f32[2,112,128]{2,1,0:T(8,128)S(1)} %fusion.k0), channel_id=1, source_target_pairs={{0,3},{1,2},{2,1},{3,0},{4,7},{5,6},{6,5},{7,4},{8,11},{9,10},{10,... | collective-permute-start | bytes 344072 | tf_op jit(solution)/shard_map/next3/ppermute | solution.py:211
  20.9 3.4 %collective-permute-start.4 = (f32[112,128]{1,0:T(8,128)S(1)}, f32[112,128]{1,0:T(8,128)S(1)}, u32[]{:S(2)}, u32[]{:S(2)}) collective-permute-start(f32[112,128]{1,0:T(8,128)S(1)} %fusion.1), channel_id=1, source_target_pairs={{0,32},{16,48},{32,0},{48,16},{64,96},{80,112},{96,64},{112,80},{1... | collective-permute-start | bytes 172040 | tf_op jit(solution)/shard_map/ylo2/ppermute | solution.py:215
  22.2 8.8 %collective-permute-start.6 = (f32[2,112,128]{2,1,0:T(8,128)S(1)}, f32[2,112,128]{2,1,0:T(8,128)S(1)}, u32[]{:S(2)}, u32[]{:S(2)}) collective-permute-start(f32[2,112,128]{2,1,0:T(8,128)S(1)} %fusion.k0), channel_id=1, source_target_pairs={{0,2},{1,3},{2,0},{3,1},{4,6},{5,7},{6,4},{7,5},{8,10},{9,11},{10,... | collective-permute-start | bytes 344072 | tf_op jit(solution)/shard_map/next2/ppermute | solution.py:211
  22.2 8.8 %collective-permute-start.5 = (f32[2,112,128]{2,1,0:T(8,128)S(1)}, f32[2,112,128]{2,1,0:T(8,128)S(1)}, u32[]{:S(2)}, u32[]{:S(2)}) collective-permute-start(f32[2,112,128]{2,1,0:T(8,128)S(1)} %fusion.k0), channel_id=1, source_target_pairs={{0,1},{1,0},{2,3},{3,2},{4,5},{5,4},{6,7},{7,6},{8,9},{9,8},{10,11... | collective-permute-start | bytes 344072 | tf_op jit(solution)/shard_map/next1/ppermute | solution.py:211
  24.3 6.8 %collective-permute-start.8 = (f32[112,128]{1,0:T(8,128)S(1)}, f32[112,128]{1,0:T(8,128)S(1)}, u32[]{:S(2)}, u32[]{:S(2)}) collective-permute-start(f32[112,128]{1,0:T(8,128)S(1)} %add.28), channel_id=1, source_target_pairs={{0,128},{16,144},{32,160},{48,176},{64,192},{80,208},{96,224},{112... | collective-permute-start | bytes 172040 | tf_op jit(solution)/shard_map/x8/ppermute | solution.py:215
  27.1 4.4 %collective-permute-start.10 = (f32[112,128]{1,0:T(8,128)S(1)}, f32[112,128]{1,0:T(8,128)S(1)}, u32[]{:S(2)}, u32[]{:S(2)}) collective-permute-start(f32[112,128]{1,0:T(8,128)S(1)} %add.28), channel_id=1, source_target_pairs={{0,192},{16,208},{32,224},{48,240},{64,128},{80,144},{96,160},{112... | collective-permute-start | bytes 172040 | tf_op jit(solution)/shard_map/x12/ppermute | solution.py:215
  28.0 3.6 %collective-permute-start.9 = (f32[112,128]{1,0:T(8,128)S(1)}, f32[112,128]{1,0:T(8,128)S(1)}, u32[]{:S(2)}, u32[]{:S(2)}) collective-permute-start(f32[112,128]{1,0:T(8,128)S(1)} %add.28), channel_id=1, source_target_pairs={{0,64},{16,80},{32,96},{48,112},{64,0},{80,16},{96,32},{112,48},{1... | collective-permute-start | bytes 172040 | tf_op jit(solution)/shard_map/x4/ppermute | solution.py:215
  31.6 5.7 %collective-permute-start.13 = (f32[112,128]{1,0:T(8,128)S(1)}, f32[112,128]{1,0:T(8,128)S(1)}, u32[]{:S(2)}, u32[]{:S(2)}) collective-permute-start(f32[112,128]{1,0:T(8,128)S(1)} %add_add_fusion), channel_id=1, source_target_pairs={{0,3},{1,2},{2,1},{3,0},{4,7},{5,6},{6,5},{7,4},{8,11},{9,10},{10,... | collective-permute-start | bytes 172040 | tf_op jit(solution)/shard_map/mean3/ppermute | solution.py:211
  33.0 5.2 %collective-permute-start.12 = (f32[112,128]{1,0:T(8,128)S(1)}, f32[112,128]{1,0:T(8,128)S(1)}, u32[]{:S(2)}, u32[]{:S(2)}) collective-permute-start(f32[112,128]{1,0:T(8,128)S(1)} %add_add_fusion), channel_id=1, source_target_pairs={{0,2},{1,3},{2,0},{3,1},{4,6},{5,7},{6,4},{7,5},{8,10},{9,11},{10,... | collective-permute-start | bytes 172040 | tf_op jit(solution)/shard_map/mean2/ppermute | solution.py:211
  33.2 5.0 %collective-permute-start.11 = (f32[112,128]{1,0:T(8,128)S(1)}, f32[112,128]{1,0:T(8,128)S(1)}, u32[]{:S(2)}, u32[]{:S(2)}) collective-permute-start(f32[112,128]{1,0:T(8,128)S(1)} %add_add_fusion), channel_id=1, source_target_pairs={{0,1},{1,0},{2,3},{3,2},{4,5},{5,4},{6,7},{7,6},{8,9},{9,8},{10,11... | collective-permute-start | bytes 172040 | tf_op jit(solution)/shard_map/mean1/ppermute | solution.py:211
  35.2 6.2 %copy-start = (f32[16,28672]{1,0:T(8,128)S(1)}, f32[16,28672]{1,0:T(8,128)}, u32[]{:S(2)}) copy-start(f32[16,28672]{1,0:T(8,128)} %base.7) | copy-start | bytes 5505028
  35.2 6.2 %copy-start.1 = (f32[16,28672]{1,0:T(8,128)S(1)}, f32[16,28672]{1,0:T(8,128)}, u32[]{:S(2)}) copy-start(f32[16,28672]{1,0:T(8,128)} %mom.3) | copy-start | bytes 5505028
  38.3 4.9 %collective-permute-start.14 = (f32[4,112,128]{2,1,0:T(8,128)S(1)}, f32[4,112,128]{2,1,0:T(8,128)S(1)}, u32[]{:S(2)}, u32[]{:S(2)}) collective-permute-start(f32[4,112,128]{2,1,0:T(8,128)S(1)} %pad_maximum_fusion.refs_0_), channel_id=1, source_target_pairs={{0,16},{16,0},{32,48},{48,32},{64,80},{80,64},{96,112},{112,96},{1... | collective-permute-start | bytes 688136 | tf_op jit(solution)/shard_map/swap1/ppermute | solution.py:215

commit v4 on v3

--- a/solution.py
+++ b/solution.py
@@ -221,11 +221,12 @@
     far2 = along_z(part2 + passed, 2, "far")
     near1 = along_z(part1, 1, "near")
     quarter = part0 + far2 + near1
-    total = quarter[0] + along_rep(quarter[1], 1, "core")
-    total = total + along_rep(total, 2, "ylo")
+    diag, ylo, beside = along_rep(quarter[1], 3, "diag"), along_rep(quarter[0], 2, "ylo"), along_rep(quarter[1], 1, "core")
+    total = quarter[0] + diag + ylo + beside
     x12, x4, x8 = (along_rep(total, s, "x") for s in (12, 4, 8))
-    next1, next3, next2 = (along_z(quarter, s, "next") for s in (1, 3, 2))
-    next1, next2, next3, x8 = lax.optimization_barrier((next1, next2, next3, x8))
+    next2, next1 = along_z(quarter, 2, "next"), along_z(quarter, 1, "next")
+    next3 = along_z(next2, 1, "relay")
+    next1, next2, x8 = lax.optimization_barrier((next1, next2, x8))
     total = total + x8 + x4 + x12
     own_pieces = [total] + [along_z(total, s, "mean") for s in range(1, PARTS)]
 

time: 45 us -> 43.9 us (0.976)
  waiting for transfers between devices: 9.82 us -> 9.19 us
  starting transfers between devices: 24 us -> 23.4 us
    ppermute x9, waiting for transfers between devices: 8.46 us -> 6.31 us  [along_z(): return lax.ppermute(value, 'fsdp', [(i, i ^ s) for i in range(shards)])]
    ppermute x6 -> x7, waiting for transfers between devices: 1.36 us -> 2.88 us  [along_rep(): return lax.ppermute(value, 'rep', [(i, i ^ s) for i in range(replicas)])]
    ppermute x6 -> x7, starting transfers between devices: 10.1 us -> 9.14 us  [along_rep(): return lax.ppermute(value, 'rep', [(i, i ^ s) for i in range(replicas)])]
    ppermute x9, starting transfers between devices: 13.8 us -> 14.3 us  [along_z(): return lax.ppermute(value, 'fsdp', [(i, i ^ s) for i in range(shards)])]
  transfers between devices with their start and end apart: 15 -> 16, of which waited for: 6 -> 6; matrix products, arithmetic and copies ran while one was open for 0% -> 0% of each run, Pallas kernels for 15% -> 15%
where the time goes in v4:
time: 43.9 us; the launch traced here: 43.8 us
  starting transfers between devices  23.4 us (53%)
  Pallas kernels  10.3 us (23%)
  waiting for transfers between devices  9.19 us (21%)
  between operations  0.77 us (2%)
    ppermute x9, starting transfers between devices, along_z(): return lax.ppermute(value, 'fsdp', [(i, i ^ s) for i in range(shards)])  14.3 us
    pallas_call x5, Pallas kernels, call(): pl.pallas_call(kernel, in_specs=in_specs, out_specs=out_specs, out_shape=...  10.3 us
    ppermute x7, starting transfers between devices, along_rep(): return lax.ppermute(value, 'rep', [(i, i ^ s) for i in range(replicas)])  9.14 us
    ppermute x9, waiting for transfers between devices, along_z(): return lax.ppermute(value, 'fsdp', [(i, i ^ s) for i in range(shards)])  6.31 us
    ppermute x7, waiting for transfers between devices, along_rep(): return lax.ppermute(value, 'rep', [(i, i ^ s) for i in range(replicas)])  2.88 us
  transfers between devices with their start and end apart: 16, of which 6 were waited for; matrix products, arithmetic and copies ran while one was open for 0% of the time, Pallas kernels for 15%

profile of v4, /device:TPU:1, one launch (start us, length us, event | category | flops | bytes accessed | tf_op | source)
XLA Modules:
  0.0 43.8 jit_solution(3344983371380902911)
XLA Ops:
  0.6 1.8 %forward.3 = (f32[1,2,112,128]{3,2,1,0:T(8,128)S(1)}, f32[1,16,7168]{2,1,0:T(8,128)S(1)}) custom-call(f32[16,28672]{1,0:T(8,128)} %base.7, bf16[1,16,28672]{2,1,0:T(8,128)(2,1)} %local.3, f32[1,16,28672]{2,1,0:T(8,128)} %err.3, bf16[512,256]{1,0:T(8,128)(2,1)} %constant.8.clone.col, f32[4,16,16]{2,1,0:T(8,128)} %constant.10.clone.rows), custom_call_target="tpu_custom_call" | custom-call | flops 117440512 | bytes 1261568 | tf_op jit(solution)/shard_map/forward/pallas_call | solution.py:168
  2.4 2.6 %collective-permute-start = (f32[2,112,128]{2,1,0:T(8,128)S(1)}, f32[2,112,128]{2,1,0:T(8,128)S(1)}, u32[]{:S(2)}, u32[]{:S(2)}) collective-permute-start(f32[2,112,128]{2,1,0:T(8,128)S(1)} %bitcast.19), channel_id=1, source_target_pairs={{0,1},{1,0},{2,3},{3,2},{4,5},{5,4},{6,7},{7,6},{8,9},{9,8},{10,11... | collective-permute-start | bytes 344072 | tf_op jit(solution)/shard_map/pass1/ppermute | solution.py:211
  4.9 3.0 %forward.2 = (f32[3,2,112,128]{3,2,1,0:T(8,128)S(1)}, f32[3,16,7168]{2,1,0:T(8,128)S(1)}) custom-call(f32[16,28672]{1,0:T(8,128)} %base.7, bf16[1,16,28672]{2,1,0:T(8,128)(2,1)} %local.3, f32[1,16,28672]{2,1,0:T(8,128)} %err.3, bf16[512,256]{1,0:T(8,128)(2,1)} %constant.8.clone.col, f32[4,16,16]{2,1,0:T(8,128)} %constant.10.clone.rows), custom_call_target="tpu_custom_call" | custom-call | flops 352321536 | bytes 3784704 | tf_op jit(solution)/shard_map/forward/pallas_call | solution.py:168
  7.9 0.0 copy-start.2
  7.9 0.0 copy-start.3
  8.0 0.0 collective-permute-done
  8.0 3.1 %collective-permute-start.1 = (f32[2,112,128]{2,1,0:T(8,128)S(1)}, f32[2,112,128]{2,1,0:T(8,128)S(1)}, u32[]{:S(2)}, u32[]{:S(2)}) collective-permute-start(f32[2,112,128]{2,1,0:T(8,128)S(1)} %bitcast_add_fusion), channel_id=1, source_target_pairs={{0,2},{1,3},{2,0},{3,1},{4,6},{5,7},{6,4},{7,5},{8,10},{9,11},{10,... | collective-permute-start | bytes 344072 | tf_op jit(solution)/shard_map/far2/ppermute | solution.py:211
  11.1 1.0 %collective-permute-start.2 = (f32[2,112,128]{2,1,0:T(8,128)S(1)}, f32[2,112,128]{2,1,0:T(8,128)S(1)}, u32[]{:S(2)}, u32[]{:S(2)}) collective-permute-start(f32[2,112,128]{2,1,0:T(8,128)S(1)} %slice_bitcast_fusion), channel_id=1, source_target_pairs={{0,1},{1,0},{2,3},{3,2},{4,5},{5,4},{6,7},{7,6},{8,9},{9,8},{10,11... | collective-permute-start | bytes 344072 | tf_op jit(solution)/shard_map/near1/ppermute | solution.py:211
  12.0 2.7 %collective-permute-done.1 = f32[2,112,128]{2,1,0:T(8,128)S(1)} collective-permute-done((f32[2,112,128]{2,1,0:T(8,128)S(1)}, f32[2,112,128]{2,1,0:T(8,128)S(1)}, u32[]{:S(2)}, u32[]{:S(2)}) %collective-permute-start.1) | collective-permute-done | bytes 114720 | tf_op jit(solution)/shard_map/far2/ppermute | solution.py:211
  14.8 1.7 %collective-permute-done.2 = f32[2,112,128]{2,1,0:T(8,128)S(1)} collective-permute-done((f32[2,112,128]{2,1,0:T(8,128)S(1)}, f32[2,112,128]{2,1,0:T(8,128)S(1)}, u32[]{:S(2)}, u32[]{:S(2)}) %collective-permute-start.2) | collective-permute-done | bytes 114720 | tf_op jit(solution)/shard_map/near1/ppermute | solution.py:211
  16.5 1.4 %collective-permute-start.4 = (f32[112,128]{1,0:T(8,128)S(1)}, f32[112,128]{1,0:T(8,128)S(1)}, u32[]{:S(2)}, u32[]{:S(2)}) collective-permute-start(f32[112,128]{1,0:T(8,128)S(1)} %get-tuple-element.39), channel_id=1, source_target_pairs={{0,32},{16,48},{32,0},{48,16},{64,96},{80,112},{96,64},{112,80},{1... | collective-permute-start | bytes 172040 | tf_op jit(solution)/shard_map/ylo2/ppermute | solution.py:215
  17.9 2.1 %collective-permute-start.5 = (f32[112,128]{1,0:T(8,128)S(1)}, f32[112,128]{1,0:T(8,128)S(1)}, u32[]{:S(2)}, u32[]{:S(2)}) collective-permute-start(f32[112,128]{1,0:T(8,128)S(1)} %get-tuple-element.40), channel_id=1, source_target_pairs={{0,16},{16,0},{32,48},{48,32},{64,80},{80,64},{96,112},{112,96},{1... | collective-permute-start | bytes 172040 | tf_op jit(solution)/shard_map/core1/ppermute | solution.py:215
  20.0 0.1 collective-permute-start.3
  20.0 0.5 %collective-permute-start.7 = (f32[2,112,128]{2,1,0:T(8,128)S(1)}, f32[2,112,128]{2,1,0:T(8,128)S(1)}, u32[]{:S(2)}, u32[]{:S(2)}) collective-permute-start(f32[2,112,128]{2,1,0:T(8,128)S(1)} %fusion.k0), channel_id=1, source_target_pairs={{0,2},{1,3},{2,0},{3,1},{4,6},{5,7},{6,4},{7,5},{8,10},{9,11},{10,... | collective-permute-start | bytes 344072 | tf_op jit(solution)/shard_map/next2/ppermute | solution.py:211
  20.6 2.2 %collective-permute-start.6 = (f32[2,112,128]{2,1,0:T(8,128)S(1)}, f32[2,112,128]{2,1,0:T(8,128)S(1)}, u32[]{:S(2)}, u32[]{:S(2)}) collective-permute-start(f32[2,112,128]{2,1,0:T(8,128)S(1)} %fusion.k0), channel_id=1, source_target_pairs={{0,1},{1,0},{2,3},{3,2},{4,5},{5,4},{6,7},{7,6},{8,9},{9,8},{10,11... | collective-permute-start | bytes 344072 | tf_op jit(solution)/shard_map/next1/ppermute | solution.py:211
  22.7 0.9 %collective-permute-done.3 = f32[112,128]{1,0:T(8,128)S(1)} collective-permute-done((f32[112,128]{1,0:T(8,128)S(1)}, f32[112,128]{1,0:T(8,128)S(1)}, u32[]{:S(2)}, u32[]{:S(2)}) %collective-permute-start.3) | collective-permute-done | bytes 57376 | tf_op jit(solution)/shard_map/diag3/ppermute | solution.py:215
  23.6 2.8 %collective-permute-start.8 = (f32[112,128]{1,0:T(8,128)S(1)}, f32[112,128]{1,0:T(8,128)S(1)}, u32[]{:S(2)}, u32[]{:S(2)}) collective-permute-start(f32[112,128]{1,0:T(8,128)S(1)} %add_add_fusion.1), channel_id=1, source_target_pairs={{0,128},{16,144},{32,160},{48,176},{64,192},{80,208},{96,224},{112... | collective-permute-start | bytes 172040 | tf_op jit(solution)/shard_map/x8/ppermute | solution.py:215
  26.5 0.8 %collective-permute-start.10 = (f32[112,128]{1,0:T(8,128)S(1)}, f32[112,128]{1,0:T(8,128)S(1)}, u32[]{:S(2)}, u32[]{:S(2)}) collective-permute-start(f32[112,128]{1,0:T(8,128)S(1)} %add_add_fusion.1), channel_id=1, source_target_pairs={{0,192},{16,208},{32,224},{48,240},{64,128},{80,144},{96,160},{112... | collective-permute-start | bytes 172040 | tf_op jit(solution)/shard_map/x12/ppermute | solution.py:215
  27.3 0.0 collective-permute-start.9
  27.3 0.9 %collective-permute-done.8 = f32[112,128]{1,0:T(8,128)S(1)} collective-permute-done((f32[112,128]{1,0:T(8,128)S(1)}, f32[112,128]{1,0:T(8,128)S(1)}, u32[]{:S(2)}, u32[]{:S(2)}) %collective-permute-start.8) | collective-permute-done | bytes 57376 | tf_op jit(solution)/shard_map/x8/ppermute | solution.py:215
  28.2 1.4 %collective-permute-start.14 = (f32[2,112,128]{2,1,0:T(8,128)S(1)}, f32[2,112,128]{2,1,0:T(8,128)S(1)}, u32[]{:S(2)}, u32[]{:S(2)}) collective-permute-start(f32[2,112,128]{2,1,0:T(8,128)S(1)} %collective-permute-done.7.k2), channel_id=1, source_target_pairs={{0,1},{1,0},{2,3},{3,2},{4,5},{5,4},{6,7},{7,6},{8,9},{9,8},{10,11... | collective-permute-start | bytes 344072 | tf_op jit(solution)/shard_map/relay1/ppermute | solution.py:211
  29.6 1.1 %collective-permute-done.10 = f32[112,128]{1,0:T(8,128)S(1)} collective-permute-done((f32[112,128]{1,0:T(8,128)S(1)}, f32[112,128]{1,0:T(8,128)S(1)}, u32[]{:S(2)}, u32[]{:S(2)}) %collective-permute-start.10) | collective-permute-done | bytes 57376 | tf_op jit(solution)/shard_map/x12/ppermute | solution.py:215
  30.7 2.5 %collective-permute-start.13 = (f32[112,128]{1,0:T(8,128)S(1)}, f32[112,128]{1,0:T(8,128)S(1)}, u32[]{:S(2)}, u32[]{:S(2)}) collective-permute-start(f32[112,128]{1,0:T(8,128)S(1)} %add_add_fusion), channel_id=1, source_target_pairs={{0,3},{1,2},{2,1},{3,0},{4,7},{5,6},{6,5},{7,4},{8,11},{9,10},{10,... | collective-permute-start | bytes 172040 | tf_op jit(solution)/shard_map/mean3/ppermute | solution.py:211
  33.2 0.0 collective-permute-start.12
  33.2 1.2 %collective-permute-start.11 = (f32[112,128]{1,0:T(8,128)S(1)}, f32[112,128]{1,0:T(8,128)S(1)}, u32[]{:S(2)}, u32[]{:S(2)}) collective-permute-start(f32[112,128]{1,0:T(8,128)S(1)} %add_add_fusion), channel_id=1, source_target_pairs={{0,1},{1,0},{2,3},{3,2},{4,5},{5,4},{6,7},{7,6},{8,9},{9,8},{10,11... | collective-permute-start | bytes 172040 | tf_op jit(solution)/shard_map/mean1/ppermute | solution.py:211
  34.4 0.0 copy-start
  34.4 0.0 copy-start.1
  34.4 2.1 %error.1 = f32[1,16,28672]{2,1,0:T(8,128)} custom-call(f32[2,112,128]{2,1,0:T(8,128)S(1)} %fusion.k0, f32[2,112,128]{2,1,0:T(8,128)S(1)} %collective-permute-done.6.k1, f32[2,112,128]{2,1,0:T(8,128)S(1)} %collective-permute-done.7.k2, f32[2,112,128]{2,1,0:T(8,128)S(1)} %collective-permute-done.14.k3, f32[1,16,7168]{2,1,0:T(8,128)S(1)} %get-tuple-element.28.field3, ...), custom_call_target="tpu_custom_call" | custom-call | flops 469762048 | bytes 3670016 | tf_op jit(solution)/shard_map/error/pallas_call | solution.py:168
  36.5 1.9 %collective-permute-done.12 = f32[112,128]{1,0:T(8,128)S(1)} collective-permute-done((f32[112,128]{1,0:T(8,128)S(1)}, f32[112,128]{1,0:T(8,128)S(1)}, u32[]{:S(2)}, u32[]{:S(2)}) %collective-permute-start.12) | collective-permute-done | bytes 57376 | tf_op jit(solution)/shard_map/mean2/ppermute | solution.py:211
  38.4 1.9 %collective-permute-start.15 = (f32[4,112,128]{2,1,0:T(8,128)S(1)}, f32[4,112,128]{2,1,0:T(8,128)S(1)}, u32[]{:S(2)}, u32[]{:S(2)}) collective-permute-start(f32[4,112,128]{2,1,0:T(8,128)S(1)} %pad_maximum_fusion.refs_0_), channel_id=1, source_target_pairs={{0,16},{16,0},{32,48},{48,32},{64,80},{80,64},{96,112},{112,96},{1... | collective-permute-start | bytes 688136 | tf_op jit(solution)/shard_map/swap1/ppermute | solution.py:215
  40.3 1.7 %update.2 = (f32[16,28672]{1,0:T(8,128)}, f32[16,28672]{1,0:T(8,128)}) custom-call(f32[16,28672]{1,0:T(8,128)S(1)} %copy-done, f32[16,28672]{1,0:T(8,128)S(1)} %copy-done.1, bf16[2,256,512]{2,1,0:T(8,128)(2,1)S(1)} %copy-done.2, f32[4,16,16]{2,1,0:T(8,128)S(1)} %copy-done.3, f32[4,112,128]{2,1,0:T(8,128)S(1)} %pad_maximum_fusion.refs_0_), custom_call_target="tpu_custom_call" | custom-call | flops 234881024 | bytes 3670016 | tf_op jit(solution)/shard_map/update/pallas_call | solution.py:168
  42.0 1.7 %update.3 = (f32[16,28672]{1,0:T(8,128)}, f32[16,28672]{1,0:T(8,128)}) custom-call(f32[16,28672]{1,0:T(8,128)S(1)} %copy-done, f32[16,28672]{1,0:T(8,128)S(1)} %copy-done.1, bf16[2,256,512]{2,1,0:T(8,128)(2,1)S(1)} %copy-done.2, f32[4,16,16]{2,1,0:T(8,128)S(1)} %copy-done.3, ...), custom_call_target="tpu_custom_call", output_to_operand_aliasing={{0}: (5, {}), {1}: (6, {})} | custom-call | flops 234881024 | bytes 3670016 | tf_op jit(solution)/shard_map/update/pallas_call | solution.py:168
  (20 shorter events, 0.1 us)
Async XLA Ops:
  2.4 5.6 %collective-permute-start = (f32[2,112,128]{2,1,0:T(8,128)S(1)}, f32[2,112,128]{2,1,0:T(8,128)S(1)}, u32[]{:S(2)}, u32[]{:S(2)}) collective-permute-start(f32[2,112,128]{2,1,0:T(8,128)S(1)} %bitcast.19), channel_id=1, source_target_pairs={{0,1},{1,0},{2,3},{3,2},{4,5},{5,4},{6,7},{7,6},{8,9},{9,8},{10,11... | collective-permute-start | bytes 344072 | tf_op jit(solution)/shard_map/pass1/ppermute | solution.py:211
  7.9 26.4 %copy-start.2 = (bf16[2,256,512]{2,1,0:T(8,128)(2,1)S(1)}, bf16[2,256,512]{2,1,0:T(8,128)(2,1)}, u32[]{:S(2)}) copy-start(bf16[2,256,512]{2,1,0:T(8,128)(2,1)} %constant.9.clone.col) | copy-start | bytes 1572868
  7.9 26.4 %copy-start.3 = (f32[4,16,16]{2,1,0:T(8,128)S(1)}, f32[4,16,16]{2,1,0:T(8,128)}, u32[]{:S(2)}) copy-start(f32[4,16,16]{2,1,0:T(8,128)} %constant.11.clone.rows) | copy-start | bytes 12292
  8.0 6.8 %collective-permute-start.1 = (f32[2,112,128]{2,1,0:T(8,128)S(1)}, f32[2,112,128]{2,1,0:T(8,128)S(1)}, u32[]{:S(2)}, u32[]{:S(2)}) collective-permute-start(f32[2,112,128]{2,1,0:T(8,128)S(1)} %bitcast_add_fusion), channel_id=1, source_target_pairs={{0,2},{1,3},{2,0},{3,1},{4,6},{5,7},{6,4},{7,5},{8,10},{9,11},{10,... | collective-permute-start | bytes 344072 | tf_op jit(solution)/shard_map/far2/ppermute | solution.py:211
  11.1 5.4 %collective-permute-start.2 = (f32[2,112,128]{2,1,0:T(8,128)S(1)}, f32[2,112,128]{2,1,0:T(8,128)S(1)}, u32[]{:S(2)}, u32[]{:S(2)}) collective-permute-start(f32[2,112,128]{2,1,0:T(8,128)S(1)} %slice_bitcast_fusion), channel_id=1, source_target_pairs={{0,1},{1,0},{2,3},{3,2},{4,5},{5,4},{6,7},{7,6},{8,9},{9,8},{10,11... | collective-permute-start | bytes 344072 | tf_op jit(solution)/shard_map/near1/ppermute | solution.py:211
  16.5 6.2 %collective-permute-start.4 = (f32[112,128]{1,0:T(8,128)S(1)}, f32[112,128]{1,0:T(8,128)S(1)}, u32[]{:S(2)}, u32[]{:S(2)}) collective-permute-start(f32[112,128]{1,0:T(8,128)S(1)} %get-tuple-element.39), channel_id=1, source_target_pairs={{0,32},{16,48},{32,0},{48,16},{64,96},{80,112},{96,64},{112,80},{1... | collective-permute-start | bytes 172040 | tf_op jit(solution)/shard_map/ylo2/ppermute | solution.py:215
  17.9 4.8 %collective-permute-start.5 = (f32[112,128]{1,0:T(8,128)S(1)}, f32[112,128]{1,0:T(8,128)S(1)}, u32[]{:S(2)}, u32[]{:S(2)}) collective-permute-start(f32[112,128]{1,0:T(8,128)S(1)} %get-tuple-element.40), channel_id=1, source_target_pairs={{0,16},{16,0},{32,48},{48,32},{64,80},{80,64},{96,112},{112,96},{1... | collective-permute-start | bytes 172040 | tf_op jit(solution)/shard_map/core1/ppermute | solution.py:215
  20.0 3.6 %collective-permute-start.3 = (f32[112,128]{1,0:T(8,128)S(1)}, f32[112,128]{1,0:T(8,128)S(1)}, u32[]{:S(2)}, u32[]{:S(2)}) collective-permute-start(f32[112,128]{1,0:T(8,128)S(1)} %get-tuple-element.40), channel_id=1, source_target_pairs={{0,48},{16,32},{32,16},{48,0},{64,112},{80,96},{96,80},{112,64},{1... | collective-permute-start | bytes 172040 | tf_op jit(solution)/shard_map/diag3/ppermute | solution.py:215
  20.0 8.2 %collective-permute-start.7 = (f32[2,112,128]{2,1,0:T(8,128)S(1)}, f32[2,112,128]{2,1,0:T(8,128)S(1)}, u32[]{:S(2)}, u32[]{:S(2)}) collective-permute-start(f32[2,112,128]{2,1,0:T(8,128)S(1)} %fusion.k0), channel_id=1, source_target_pairs={{0,2},{1,3},{2,0},{3,1},{4,6},{5,7},{6,4},{7,5},{8,10},{9,11},{10,... | collective-permute-start | bytes 344072 | tf_op jit(solution)/shard_map/next2/ppermute | solution.py:211
  20.6 7.7 %collective-permute-start.6 = (f32[2,112,128]{2,1,0:T(8,128)S(1)}, f32[2,112,128]{2,1,0:T(8,128)S(1)}, u32[]{:S(2)}, u32[]{:S(2)}) collective-permute-start(f32[2,112,128]{2,1,0:T(8,128)S(1)} %fusion.k0), channel_id=1, source_target_pairs={{0,1},{1,0},{2,3},{3,2},{4,5},{5,4},{6,7},{7,6},{8,9},{9,8},{10,11... | collective-permute-start | bytes 344072 | tf_op jit(solution)/shard_map/next1/ppermute | solution.py:211
  23.6 4.6 %collective-permute-start.8 = (f32[112,128]{1,0:T(8,128)S(1)}, f32[112,128]{1,0:T(8,128)S(1)}, u32[]{:S(2)}, u32[]{:S(2)}) collective-permute-start(f32[112,128]{1,0:T(8,128)S(1)} %add_add_fusion.1), channel_id=1, source_target_pairs={{0,128},{16,144},{32,160},{48,176},{64,192},{80,208},{96,224},{112... | collective-permute-start | bytes 172040 | tf_op jit(solution)/shard_map/x8/ppermute | solution.py:215
  26.5 4.2 %collective-permute-start.10 = (f32[112,128]{1,0:T(8,128)S(1)}, f32[112,128]{1,0:T(8,128)S(1)}, u32[]{:S(2)}, u32[]{:S(2)}) collective-permute-start(f32[112,128]{1,0:T(8,128)S(1)} %add_add_fusion.1), channel_id=1, source_target_pairs={{0,192},{16,208},{32,224},{48,240},{64,128},{80,144},{96,160},{112... | collective-permute-start | bytes 172040 | tf_op jit(solution)/shard_map/x12/ppermute | solution.py:215
  27.3 3.4 %collective-permute-start.9 = (f32[112,128]{1,0:T(8,128)S(1)}, f32[112,128]{1,0:T(8,128)S(1)}, u32[]{:S(2)}, u32[]{:S(2)}) collective-permute-start(f32[112,128]{1,0:T(8,128)S(1)} %add_add_fusion.1), channel_id=1, source_target_pairs={{0,64},{16,80},{32,96},{48,112},{64,0},{80,16},{96,32},{112,48},{1... | collective-permute-start | bytes 172040 | tf_op jit(solution)/shard_map/x4/ppermute | solution.py:215
  28.2 6.1 %collective-permute-start.14 = (f32[2,112,128]{2,1,0:T(8,128)S(1)}, f32[2,112,128]{2,1,0:T(8,128)S(1)}, u32[]{:S(2)}, u32[]{:S(2)}) collective-permute-start(f32[2,112,128]{2,1,0:T(8,128)S(1)} %collective-permute-done.7.k2), channel_id=1, source_target_pairs={{0,1},{1,0},{2,3},{3,2},{4,5},{5,4},{6,7},{7,6},{8,9},{9,8},{10,11... | collective-permute-start | bytes 344072 | tf_op jit(solution)/shard_map/relay1/ppermute | solution.py:211
  30.7 5.8 %collective-permute-start.13 = (f32[112,128]{1,0:T(8,128)S(1)}, f32[112,128]{1,0:T(8,128)S(1)}, u32[]{:S(2)}, u32[]{:S(2)}) collective-permute-start(f32[112,128]{1,0:T(8,128)S(1)} %add_add_fusion), channel_id=1, source_target_pairs={{0,3},{1,2},{2,1},{3,0},{4,7},{5,6},{6,5},{7,4},{8,11},{9,10},{10,... | collective-permute-start | bytes 172040 | tf_op jit(solution)/shard_map/mean3/ppermute | solution.py:211
  33.2 5.1 %collective-permute-start.12 = (f32[112,128]{1,0:T(8,128)S(1)}, f32[112,128]{1,0:T(8,128)S(1)}, u32[]{:S(2)}, u32[]{:S(2)}) collective-permute-start(f32[112,128]{1,0:T(8,128)S(1)} %add_add_fusion), channel_id=1, source_target_pairs={{0,2},{1,3},{2,0},{3,1},{4,6},{5,7},{6,4},{7,5},{8,10},{9,11},{10,... | collective-permute-start | bytes 172040 | tf_op jit(solution)/shard_map/mean2/ppermute | solution.py:211
  33.2 5.1 %collective-permute-start.11 = (f32[112,128]{1,0:T(8,128)S(1)}, f32[112,128]{1,0:T(8,128)S(1)}, u32[]{:S(2)}, u32[]{:S(2)}) collective-permute-start(f32[112,128]{1,0:T(8,128)S(1)} %add_add_fusion), channel_id=1, source_target_pairs={{0,1},{1,0},{2,3},{3,2},{4,5},{5,4},{6,7},{7,6},{8,9},{9,8},{10,11... | collective-permute-start | bytes 172040 | tf_op jit(solution)/shard_map/mean1/ppermute | solution.py:211
  34.4 5.9 %copy-start = (f32[16,28672]{1,0:T(8,128)S(1)}, f32[16,28672]{1,0:T(8,128)}, u32[]{:S(2)}) copy-start(f32[16,28672]{1,0:T(8,128)} %base.7) | copy-start | bytes 5505028
  34.4 5.9 %copy-start.1 = (f32[16,28672]{1,0:T(8,128)S(1)}, f32[16,28672]{1,0:T(8,128)}, u32[]{:S(2)}) copy-start(f32[16,28672]{1,0:T(8,128)} %mom.3) | copy-start | bytes 5505028
  38.4 3.7 %collective-permute-start.15 = (f32[4,112,128]{2,1,0:T(8,128)S(1)}, f32[4,112,128]{2,1,0:T(8,128)S(1)}, u32[]{:S(2)}, u32[]{:S(2)}) collective-permute-start(f32[4,112,128]{2,1,0:T(8,128)S(1)} %pad_maximum_fusion.refs_0_), channel_id=1, source_target_pairs={{0,16},{16,0},{32,48},{48,32},{64,80},{80,64},{96,112},{112,96},{1... | collective-permute-start | bytes 688136 | tf_op jit(solution)/shard_map/swap1/ppermute | solution.py:215

commit v5 on v4

--- a/solution.py
+++ b/solution.py
@@ -120,10 +120,10 @@
     return dot(both, col[0]) + dot(both, col[1])
 
 
-def error_kernel(k0, k1, k2, k3, field3, fields, col, rows, out, out_v, sems):
+def error_kernel(k0, k1, k2, k3, field3, fields, field0, col, rows, out, out_v, sems):
     part, core = position()
     width = out.shape[2]
-    order = ((k0, fields.at[2]), (k1, fields.at[1]), (k2, fields.at[0]), (k3, field3.at[0]))
+    order = ((k0, field0.at[0]), (k1, fields.at[1]), (k2, fields.at[0]), (k3, field3.at[0]))
     coeffs = jnp.concatenate([k[h] for k, _ in order for h in (core, 1 - core)], axis=0)
     kept = inverse_rows(rows[part], col, coeffs)
     count = coeffs.shape[0] // PARTS
@@ -216,10 +216,11 @@
 
     (part3,), field3 = forward(3)
     passed = along_z(part3, 1, "pass")
-    (part2, part1, part0), fields = forward(2, 1, 0)
+    (part2, part1), fields = forward(2, 1)
     passed, part1 = lax.optimization_barrier((passed, part1))
     far2 = along_z(part2 + passed, 2, "far")
     near1 = along_z(part1, 1, "near")
+    (part0,), field0 = forward(0)
     quarter = part0 + far2 + near1
     diag, ylo, beside = along_rep(quarter[1], 3, "diag"), along_rep(quarter[0], 2, "ylo"), along_rep(quarter[1], 1, "core")
     total = quarter[0] + diag + ylo + beside
@@ -232,8 +233,8 @@
 
     new_error = call(
         error_kernel, "error",
-        (quarter, next1, next2, next3, field3, fields, col_inv, rows_inv),
-        [VMEM] * 8,
+        (quarter, next1, next2, next3, field3, fields, field0, col_inv, rows_inv),
+        [VMEM] * 9,
         HBM, f32(1, rows, width),
         [buffer(), pltpu.SemaphoreType.DMA((PARTS,))],
         flops=cells * 1024, moved=cells * 8,

time: 43.9 us -> 43.9 us (level)
  waiting for transfers between devices: 9.19 us -> 5 us
  starting transfers between devices: 23.4 us -> 26.4 us
  Pallas kernels: 10.3 us -> 11.4 us
    ppermute x9, waiting for transfers between devices: 6.31 us -> 2.85 us  [along_z(): return lax.ppermute(value, 'fsdp', [(i, i ^ s) for i in range(shards)])]
    ppermute x7, starting transfers between devices: 9.14 us -> 11 us  [along_rep(): return lax.ppermute(value, 'rep', [(i, i ^ s) for i in range(replicas)])]
    ppermute x9, starting transfers between devices: 14.3 us -> 15.5 us  [along_z(): return lax.ppermute(value, 'fsdp', [(i, i ^ s) for i in range(shards)])]
    pallas_call x5 -> x6, Pallas kernels: 10.3 us -> 11.4 us  [call(): pl.pallas_call(kernel, in_specs=in_specs, out_specs=out_specs, out_shape=...]
    ppermute x7, waiting for transfers between devices: 2.88 us -> 2.14 us  [along_rep(): return lax.ppermute(value, 'rep', [(i, i ^ s) for i in range(replicas)])]
  transfers between devices with their start and end apart: 16 -> 16, of which waited for: 6 -> 6; matrix products, arithmetic and copies ran while one was open for 0% -> 0% of each run, Pallas kernels for 15% -> 18%
where the time goes in v5:
time: 43.9 us; the launch traced here: 43.7 us
  starting transfers between devices  26.4 us (60%)
  Pallas kernels  11.4 us (26%)
  waiting for transfers between devices  5 us (11%)
  between operations  0.78 us (2%)
    ppermute x9, starting transfers between devices, along_z(): return lax.ppermute(value, 'fsdp', [(i, i ^ s) for i in range(shards)])  15.5 us
    pallas_call x6, Pallas kernels, call(): pl.pallas_call(kernel, in_specs=in_specs, out_specs=out_specs, out_shape=...  11.4 us
    ppermute x7, starting transfers between devices, along_rep(): return lax.ppermute(value, 'rep', [(i, i ^ s) for i in range(replicas)])  11 us
    ppermute x9, waiting for transfers between devices, along_z(): return lax.ppermute(value, 'fsdp', [(i, i ^ s) for i in range(shards)])  2.85 us
    ppermute x7, waiting for transfers between devices, along_rep(): return lax.ppermute(value, 'rep', [(i, i ^ s) for i in range(replicas)])  2.14 us
  transfers between devices with their start and end apart: 16, of which 6 were waited for; matrix products, arithmetic and copies ran while one was open for 0% of the time, Pallas kernels for 18%

profile of v5, /device:TPU:1, one launch (start us, length us, event | category | flops | bytes accessed | tf_op | source)
XLA Modules:
  0.0 43.7 jit_solution(643697498432625608)
XLA Ops:
  0.6 1.8 %forward.5 = (f32[1,2,112,128]{3,2,1,0:T(8,128)S(1)}, f32[1,16,7168]{2,1,0:T(8,128)S(1)}) custom-call(f32[16,28672]{1,0:T(8,128)} %base.9, bf16[1,16,28672]{2,1,0:T(8,128)(2,1)} %local.5, f32[1,16,28672]{2,1,0:T(8,128)} %err.5, bf16[512,256]{1,0:T(8,128)(2,1)} %constant.8.clone.col, f32[4,16,16]{2,1,0:T(8,128)} %constant.10.clone.rows), custom_call_target="tpu_custom_call" | custom-call | flops 117440512 | bytes 1261568 | tf_op jit(solution)/shard_map/forward/pallas_call | solution.py:168
  2.4 2.6 %collective-permute-start = (f32[2,112,128]{2,1,0:T(8,128)S(1)}, f32[2,112,128]{2,1,0:T(8,128)S(1)}, u32[]{:S(2)}, u32[]{:S(2)}) collective-permute-start(f32[2,112,128]{2,1,0:T(8,128)S(1)} %bitcast.19), channel_id=1, source_target_pairs={{0,1},{1,0},{2,3},{3,2},{4,5},{5,4},{6,7},{7,6},{8,9},{9,8},{10,11... | collective-permute-start | bytes 344072 | tf_op jit(solution)/shard_map/pass1/ppermute | solution.py:211
  4.9 2.4 %forward.4 = (f32[2,2,112,128]{3,2,1,0:T(8,128)S(1)}, f32[2,16,7168]{2,1,0:T(8,128)S(1)}) custom-call(f32[16,28672]{1,0:T(8,128)} %base.9, bf16[1,16,28672]{2,1,0:T(8,128)(2,1)} %local.5, f32[1,16,28672]{2,1,0:T(8,128)} %err.5, bf16[512,256]{1,0:T(8,128)(2,1)} %constant.8.clone.col, f32[4,16,16]{2,1,0:T(8,128)} %constant.10.clone.rows), custom_call_target="tpu_custom_call" | custom-call | flops 234881024 | bytes 2523136 | tf_op jit(solution)/shard_map/forward/pallas_call | solution.py:168
  7.3 0.0 collective-permute-done
  7.4 0.0 copy-start.2
  7.4 0.0 copy-start.3
  7.4 3.4 %collective-permute-start.1 = (f32[2,112,128]{2,1,0:T(8,128)S(1)}, f32[2,112,128]{2,1,0:T(8,128)S(1)}, u32[]{:S(2)}, u32[]{:S(2)}) collective-permute-start(f32[2,112,128]{2,1,0:T(8,128)S(1)} %bitcast_add_fusion), channel_id=1, source_target_pairs={{0,2},{1,3},{2,0},{3,1},{4,6},{5,7},{6,4},{7,5},{8,10},{9,11},{10,... | collective-permute-start | bytes 344072 | tf_op jit(solution)/shard_map/far2/ppermute | solution.py:211
  10.8 1.3 %collective-permute-start.2 = (f32[2,112,128]{2,1,0:T(8,128)S(1)}, f32[2,112,128]{2,1,0:T(8,128)S(1)}, u32[]{:S(2)}, u32[]{:S(2)}) collective-permute-start(f32[2,112,128]{2,1,0:T(8,128)S(1)} %slice_bitcast_fusion), channel_id=1, source_target_pairs={{0,1},{1,0},{2,3},{3,2},{4,5},{5,4},{6,7},{7,6},{8,9},{9,8},{10,11... | collective-permute-start | bytes 344072 | tf_op jit(solution)/shard_map/near1/ppermute | solution.py:211
  12.1 1.7 %forward.3 = (f32[1,2,112,128]{3,2,1,0:T(8,128)S(1)}, f32[1,16,7168]{2,1,0:T(8,128)S(1)}) custom-call(f32[16,28672]{1,0:T(8,128)} %base.9, bf16[1,16,28672]{2,1,0:T(8,128)(2,1)} %local.5, f32[1,16,28672]{2,1,0:T(8,128)} %err.5, bf16[512,256]{1,0:T(8,128)(2,1)} %constant.8.clone.col, f32[4,16,16]{2,1,0:T(8,128)} %constant.10.clone.rows), custom_call_target="tpu_custom_call" | custom-call | flops 117440512 | bytes 1261568 | tf_op jit(solution)/shard_map/forward/pallas_call | solution.py:168
  13.8 0.5 %collective-permute-done.1 = f32[2,112,128]{2,1,0:T(8,128)S(1)} collective-permute-done((f32[2,112,128]{2,1,0:T(8,128)S(1)}, f32[2,112,128]{2,1,0:T(8,128)S(1)}, u32[]{:S(2)}, u32[]{:S(2)}) %collective-permute-start.1) | collective-permute-done | bytes 114720 | tf_op jit(solution)/shard_map/far2/ppermute | solution.py:211
  14.3 0.9 %collective-permute-done.2 = f32[2,112,128]{2,1,0:T(8,128)S(1)} collective-permute-done((f32[2,112,128]{2,1,0:T(8,128)S(1)}, f32[2,112,128]{2,1,0:T(8,128)S(1)}, u32[]{:S(2)}, u32[]{:S(2)}) %collective-permute-start.2) | collective-permute-done | bytes 114720 | tf_op jit(solution)/shard_map/near1/ppermute | solution.py:211
  15.3 1.8 %collective-permute-start.4 = (f32[112,128]{1,0:T(8,128)S(1)}, f32[112,128]{1,0:T(8,128)S(1)}, u32[]{:S(2)}, u32[]{:S(2)}) collective-permute-start(f32[112,128]{1,0:T(8,128)S(1)} %get-tuple-element.43), channel_id=1, source_target_pairs={{0,32},{16,48},{32,0},{48,16},{64,96},{80,112},{96,64},{112,80},{1... | collective-permute-start | bytes 172040 | tf_op jit(solution)/shard_map/ylo2/ppermute | solution.py:215
  17.0 2.4 %collective-permute-start.5 = (f32[112,128]{1,0:T(8,128)S(1)}, f32[112,128]{1,0:T(8,128)S(1)}, u32[]{:S(2)}, u32[]{:S(2)}) collective-permute-start(f32[112,128]{1,0:T(8,128)S(1)} %get-tuple-element.44), channel_id=1, source_target_pairs={{0,16},{16,0},{32,48},{48,32},{64,80},{80,64},{96,112},{112,96},{1... | collective-permute-start | bytes 172040 | tf_op jit(solution)/shard_map/core1/ppermute | solution.py:215
  19.5 0.2 collective-permute-start.3
  19.7 0.7 %collective-permute-start.7 = (f32[2,112,128]{2,1,0:T(8,128)S(1)}, f32[2,112,128]{2,1,0:T(8,128)S(1)}, u32[]{:S(2)}, u32[]{:S(2)}) collective-permute-start(f32[2,112,128]{2,1,0:T(8,128)S(1)} %fusion.k0), channel_id=1, source_target_pairs={{0,2},{1,3},{2,0},{3,1},{4,6},{5,7},{6,4},{7,5},{8,10},{9,11},{10,... | collective-permute-start | bytes 344072 | tf_op jit(solution)/shard_map/next2/ppermute | solution.py:211
  20.4 2.2 %collective-permute-start.6 = (f32[2,112,128]{2,1,0:T(8,128)S(1)}, f32[2,112,128]{2,1,0:T(8,128)S(1)}, u32[]{:S(2)}, u32[]{:S(2)}) collective-permute-start(f32[2,112,128]{2,1,0:T(8,128)S(1)} %fusion.k0), channel_id=1, source_target_pairs={{0,1},{1,0},{2,3},{3,2},{4,5},{5,4},{6,7},{7,6},{8,9},{9,8},{10,11... | collective-permute-start | bytes 344072 | tf_op jit(solution)/shard_map/next1/ppermute | solution.py:211
  22.7 0.4 collective-permute-done.3
  23.1 2.8 %collective-permute-start.8 = (f32[112,128]{1,0:T(8,128)S(1)}, f32[112,128]{1,0:T(8,128)S(1)}, u32[]{:S(2)}, u32[]{:S(2)}) collective-permute-start(f32[112,128]{1,0:T(8,128)S(1)} %add_add_fusion.1), channel_id=1, source_target_pairs={{0,128},{16,144},{32,160},{48,176},{64,192},{80,208},{96,224},{112... | collective-permute-start | bytes 172040 | tf_op jit(solution)/shard_map/x8/ppermute | solution.py:215
  25.9 0.9 %collective-permute-start.10 = (f32[112,128]{1,0:T(8,128)S(1)}, f32[112,128]{1,0:T(8,128)S(1)}, u32[]{:S(2)}, u32[]{:S(2)}) collective-permute-start(f32[112,128]{1,0:T(8,128)S(1)} %add_add_fusion.1), channel_id=1, source_target_pairs={{0,192},{16,208},{32,224},{48,240},{64,128},{80,144},{96,160},{112... | collective-permute-start | bytes 172040 | tf_op jit(solution)/shard_map/x12/ppermute | solution.py:215
  26.8 0.0 collective-permute-start.9
  26.8 0.9 %collective-permute-done.8 = f32[112,128]{1,0:T(8,128)S(1)} collective-permute-done((f32[112,128]{1,0:T(8,128)S(1)}, f32[112,128]{1,0:T(8,128)S(1)}, u32[]{:S(2)}, u32[]{:S(2)}) %collective-permute-start.8) | collective-permute-done | bytes 57376 | tf_op jit(solution)/shard_map/x8/ppermute | solution.py:215
  27.7 1.6 %collective-permute-start.14 = (f32[2,112,128]{2,1,0:T(8,128)S(1)}, f32[2,112,128]{2,1,0:T(8,128)S(1)}, u32[]{:S(2)}, u32[]{:S(2)}) collective-permute-start(f32[2,112,128]{2,1,0:T(8,128)S(1)} %collective-permute-done.7.k2), channel_id=1, source_target_pairs={{0,1},{1,0},{2,3},{3,2},{4,5},{5,4},{6,7},{7,6},{8,9},{9,8},{10,11... | collective-permute-start | bytes 344072 | tf_op jit(solution)/shard_map/relay1/ppermute | solution.py:211
  29.3 0.8 %collective-permute-done.10 = f32[112,128]{1,0:T(8,128)S(1)} collective-permute-done((f32[112,128]{1,0:T(8,128)S(1)}, f32[112,128]{1,0:T(8,128)S(1)}, u32[]{:S(2)}, u32[]{:S(2)}) %collective-permute-start.10) | collective-permute-done | bytes 57376 | tf_op jit(solution)/shard_map/x12/ppermute | solution.py:215
  30.2 3.0 %collective-permute-start.13 = (f32[112,128]{1,0:T(8,128)S(1)}, f32[112,128]{1,0:T(8,128)S(1)}, u32[]{:S(2)}, u32[]{:S(2)}) collective-permute-start(f32[112,128]{1,0:T(8,128)S(1)} %add_add_fusion), channel_id=1, source_target_pairs={{0,3},{1,2},{2,1},{3,0},{4,7},{5,6},{6,5},{7,4},{8,11},{9,10},{10,... | collective-permute-start | bytes 172040 | tf_op jit(solution)/shard_map/mean3/ppermute | solution.py:211
  33.1 0.7 %collective-permute-start.11 = (f32[112,128]{1,0:T(8,128)S(1)}, f32[112,128]{1,0:T(8,128)S(1)}, u32[]{:S(2)}, u32[]{:S(2)}) collective-permute-start(f32[112,128]{1,0:T(8,128)S(1)} %add_add_fusion), channel_id=1, source_target_pairs={{0,1},{1,0},{2,3},{3,2},{4,5},{5,4},{6,7},{7,6},{8,9},{9,8},{10,11... | collective-permute-start | bytes 172040 | tf_op jit(solution)/shard_map/mean1/ppermute | solution.py:211
  33.8 0.0 copy-start
  33.8 0.0 copy-start.1
  33.9 2.1 %error.1 = f32[1,16,28672]{2,1,0:T(8,128)} custom-call(f32[2,112,128]{2,1,0:T(8,128)S(1)} %fusion.k0, f32[2,112,128]{2,1,0:T(8,128)S(1)} %collective-permute-done.6.k1, f32[2,112,128]{2,1,0:T(8,128)S(1)} %collective-permute-done.7.k2, f32[2,112,128]{2,1,0:T(8,128)S(1)} %collective-permute-done.14.k3, f32[1,16,7168]{2,1,0:T(8,128)S(1)} %get-tuple-element.31.field3, ...), custom_call_target="tpu_custom_call" | custom-call | flops 469762048 | bytes 3670016 | tf_op jit(solution)/shard_map/error/pallas_call | solution.py:168
  35.9 1.4 %collective-permute-done.12 = f32[112,128]{1,0:T(8,128)S(1)} collective-permute-done((f32[112,128]{1,0:T(8,128)S(1)}, f32[112,128]{1,0:T(8,128)S(1)}, u32[]{:S(2)}, u32[]{:S(2)}) %collective-permute-start.12) | collective-permute-done | bytes 57376 | tf_op jit(solution)/shard_map/mean2/ppermute | solution.py:211
  37.4 2.8 %collective-permute-start.15 = (f32[4,112,128]{2,1,0:T(8,128)S(1)}, f32[4,112,128]{2,1,0:T(8,128)S(1)}, u32[]{:S(2)}, u32[]{:S(2)}) collective-permute-start(f32[4,112,128]{2,1,0:T(8,128)S(1)} %pad_maximum_fusion.refs_0_), channel_id=1, source_target_pairs={{0,16},{16,0},{32,48},{48,32},{64,80},{80,64},{96,112},{112,96},{1... | collective-permute-start | bytes 688136 | tf_op jit(solution)/shard_map/swap1/ppermute | solution.py:215
  40.2 1.7 %update.2 = (f32[16,28672]{1,0:T(8,128)}, f32[16,28672]{1,0:T(8,128)}) custom-call(f32[16,28672]{1,0:T(8,128)S(1)} %copy-done, f32[16,28672]{1,0:T(8,128)S(1)} %copy-done.1, bf16[2,256,512]{2,1,0:T(8,128)(2,1)S(1)} %copy-done.2, f32[4,16,16]{2,1,0:T(8,128)S(1)} %copy-done.3, f32[4,112,128]{2,1,0:T(8,128)S(1)} %pad_maximum_fusion.refs_0_), custom_call_target="tpu_custom_call" | custom-call | flops 234881024 | bytes 3670016 | tf_op jit(solution)/shard_map/update/pallas_call | solution.py:168
  42.0 1.7 %update.3 = (f32[16,28672]{1,0:T(8,128)}, f32[16,28672]{1,0:T(8,128)}) custom-call(f32[16,28672]{1,0:T(8,128)S(1)} %copy-done, f32[16,28672]{1,0:T(8,128)S(1)} %copy-done.1, bf16[2,256,512]{2,1,0:T(8,128)(2,1)S(1)} %copy-done.2, f32[4,16,16]{2,1,0:T(8,128)S(1)} %copy-done.3, ...), custom_call_target="tpu_custom_call", output_to_operand_aliasing={{0}: (5, {}), {1}: (6, {})} | custom-call | flops 234881024 | bytes 3670016 | tf_op jit(solution)/shard_map/update/pallas_call | solution.py:168
  (21 shorter events, 0.1 us)
Async XLA Ops:
  2.4 4.9 %collective-permute-start = (f32[2,112,128]{2,1,0:T(8,128)S(1)}, f32[2,112,128]{2,1,0:T(8,128)S(1)}, u32[]{:S(2)}, u32[]{:S(2)}) collective-permute-start(f32[2,112,128]{2,1,0:T(8,128)S(1)} %bitcast.19), channel_id=1, source_target_pairs={{0,1},{1,0},{2,3},{3,2},{4,5},{5,4},{6,7},{7,6},{8,9},{9,8},{10,11... | collective-permute-start | bytes 344072 | tf_op jit(solution)/shard_map/pass1/ppermute | solution.py:211
  7.4 26.5 %copy-start.2 = (bf16[2,256,512]{2,1,0:T(8,128)(2,1)S(1)}, bf16[2,256,512]{2,1,0:T(8,128)(2,1)}, u32[]{:S(2)}) copy-start(bf16[2,256,512]{2,1,0:T(8,128)(2,1)} %constant.9.clone.col) | copy-start | bytes 1572868
  7.4 26.5 %copy-start.3 = (f32[4,16,16]{2,1,0:T(8,128)S(1)}, f32[4,16,16]{2,1,0:T(8,128)}, u32[]{:S(2)}) copy-start(f32[4,16,16]{2,1,0:T(8,128)} %constant.11.clone.rows) | copy-start | bytes 12292
  7.4 7.0 %collective-permute-start.1 = (f32[2,112,128]{2,1,0:T(8,128)S(1)}, f32[2,112,128]{2,1,0:T(8,128)S(1)}, u32[]{:S(2)}, u32[]{:S(2)}) collective-permute-start(f32[2,112,128]{2,1,0:T(8,128)S(1)} %bitcast_add_fusion), channel_id=1, source_target_pairs={{0,2},{1,3},{2,0},{3,1},{4,6},{5,7},{6,4},{7,5},{8,10},{9,11},{10,... | collective-permute-start | bytes 344072 | tf_op jit(solution)/shard_map/far2/ppermute | solution.py:211
  10.8 4.4 %collective-permute-start.2 = (f32[2,112,128]{2,1,0:T(8,128)S(1)}, f32[2,112,128]{2,1,0:T(8,128)S(1)}, u32[]{:S(2)}, u32[]{:S(2)}) collective-permute-start(f32[2,112,128]{2,1,0:T(8,128)S(1)} %slice_bitcast_fusion), channel_id=1, source_target_pairs={{0,1},{1,0},{2,3},{3,2},{4,5},{5,4},{6,7},{7,6},{8,9},{9,8},{10,11... | collective-permute-start | bytes 344072 | tf_op jit(solution)/shard_map/near1/ppermute | solution.py:211
  15.3 7.4 %collective-permute-start.4 = (f32[112,128]{1,0:T(8,128)S(1)}, f32[112,128]{1,0:T(8,128)S(1)}, u32[]{:S(2)}, u32[]{:S(2)}) collective-permute-start(f32[112,128]{1,0:T(8,128)S(1)} %get-tuple-element.43), channel_id=1, source_target_pairs={{0,32},{16,48},{32,0},{48,16},{64,96},{80,112},{96,64},{112,80},{1... | collective-permute-start | bytes 172040 | tf_op jit(solution)/shard_map/ylo2/ppermute | solution.py:215
  17.0 5.7 %collective-permute-start.5 = (f32[112,128]{1,0:T(8,128)S(1)}, f32[112,128]{1,0:T(8,128)S(1)}, u32[]{:S(2)}, u32[]{:S(2)}) collective-permute-start(f32[112,128]{1,0:T(8,128)S(1)} %get-tuple-element.44), channel_id=1, source_target_pairs={{0,16},{16,0},{32,48},{48,32},{64,80},{80,64},{96,112},{112,96},{1... | collective-permute-start | bytes 172040 | tf_op jit(solution)/shard_map/core1/ppermute | solution.py:215
  19.5 3.6 %collective-permute-start.3 = (f32[112,128]{1,0:T(8,128)S(1)}, f32[112,128]{1,0:T(8,128)S(1)}, u32[]{:S(2)}, u32[]{:S(2)}) collective-permute-start(f32[112,128]{1,0:T(8,128)S(1)} %get-tuple-element.44), channel_id=1, source_target_pairs={{0,48},{16,32},{32,16},{48,0},{64,112},{80,96},{96,80},{112,64},{1... | collective-permute-start | bytes 172040 | tf_op jit(solution)/shard_map/diag3/ppermute | solution.py:215
  19.7 8.0 %collective-permute-start.7 = (f32[2,112,128]{2,1,0:T(8,128)S(1)}, f32[2,112,128]{2,1,0:T(8,128)S(1)}, u32[]{:S(2)}, u32[]{:S(2)}) collective-permute-start(f32[2,112,128]{2,1,0:T(8,128)S(1)} %fusion.k0), channel_id=1, source_target_pairs={{0,2},{1,3},{2,0},{3,1},{4,6},{5,7},{6,4},{7,5},{8,10},{9,11},{10,... | collective-permute-start | bytes 344072 | tf_op jit(solution)/shard_map/next2/ppermute | solution.py:211
  20.4 7.3 %collective-permute-start.6 = (f32[2,112,128]{2,1,0:T(8,128)S(1)}, f32[2,112,128]{2,1,0:T(8,128)S(1)}, u32[]{:S(2)}, u32[]{:S(2)}) collective-permute-start(f32[2,112,128]{2,1,0:T(8,128)S(1)} %fusion.k0), channel_id=1, source_target_pairs={{0,1},{1,0},{2,3},{3,2},{4,5},{5,4},{6,7},{7,6},{8,9},{9,8},{10,11... | collective-permute-start | bytes 344072 | tf_op jit(solution)/shard_map/next1/ppermute | solution.py:211
  23.1 4.6 %collective-permute-start.8 = (f32[112,128]{1,0:T(8,128)S(1)}, f32[112,128]{1,0:T(8,128)S(1)}, u32[]{:S(2)}, u32[]{:S(2)}) collective-permute-start(f32[112,128]{1,0:T(8,128)S(1)} %add_add_fusion.1), channel_id=1, source_target_pairs={{0,128},{16,144},{32,160},{48,176},{64,192},{80,208},{96,224},{112... | collective-permute-start | bytes 172040 | tf_op jit(solution)/shard_map/x8/ppermute | solution.py:215
  25.9 4.2 %collective-permute-start.10 = (f32[112,128]{1,0:T(8,128)S(1)}, f32[112,128]{1,0:T(8,128)S(1)}, u32[]{:S(2)}, u32[]{:S(2)}) collective-permute-start(f32[112,128]{1,0:T(8,128)S(1)} %add_add_fusion.1), channel_id=1, source_target_pairs={{0,192},{16,208},{32,224},{48,240},{64,128},{80,144},{96,160},{112... | collective-permute-start | bytes 172040 | tf_op jit(solution)/shard_map/x12/ppermute | solution.py:215
  26.8 3.4 %collective-permute-start.9 = (f32[112,128]{1,0:T(8,128)S(1)}, f32[112,128]{1,0:T(8,128)S(1)}, u32[]{:S(2)}, u32[]{:S(2)}) collective-permute-start(f32[112,128]{1,0:T(8,128)S(1)} %add_add_fusion.1), channel_id=1, source_target_pairs={{0,64},{16,80},{32,96},{48,112},{64,0},{80,16},{96,32},{112,48},{1... | collective-permute-start | bytes 172040 | tf_op jit(solution)/shard_map/x4/ppermute | solution.py:215
  27.7 6.1 %collective-permute-start.14 = (f32[2,112,128]{2,1,0:T(8,128)S(1)}, f32[2,112,128]{2,1,0:T(8,128)S(1)}, u32[]{:S(2)}, u32[]{:S(2)}) collective-permute-start(f32[2,112,128]{2,1,0:T(8,128)S(1)} %collective-permute-done.7.k2), channel_id=1, source_target_pairs={{0,1},{1,0},{2,3},{3,2},{4,5},{5,4},{6,7},{7,6},{8,9},{9,8},{10,11... | collective-permute-start | bytes 344072 | tf_op jit(solution)/shard_map/relay1/ppermute | solution.py:211
  30.2 5.8 %collective-permute-start.13 = (f32[112,128]{1,0:T(8,128)S(1)}, f32[112,128]{1,0:T(8,128)S(1)}, u32[]{:S(2)}, u32[]{:S(2)}) collective-permute-start(f32[112,128]{1,0:T(8,128)S(1)} %add_add_fusion), channel_id=1, source_target_pairs={{0,3},{1,2},{2,1},{3,0},{4,7},{5,6},{6,5},{7,4},{8,11},{9,10},{10,... | collective-permute-start | bytes 172040 | tf_op jit(solution)/shard_map/mean3/ppermute | solution.py:211
  33.1 4.2 %collective-permute-start.12 = (f32[112,128]{1,0:T(8,128)S(1)}, f32[112,128]{1,0:T(8,128)S(1)}, u32[]{:S(2)}, u32[]{:S(2)}) collective-permute-start(f32[112,128]{1,0:T(8,128)S(1)} %add_add_fusion), channel_id=1, source_target_pairs={{0,2},{1,3},{2,0},{3,1},{4,6},{5,7},{6,4},{7,5},{8,10},{9,11},{10,... | collective-permute-start | bytes 172040 | tf_op jit(solution)/shard_map/mean2/ppermute | solution.py:211
  33.1 4.2 %collective-permute-start.11 = (f32[112,128]{1,0:T(8,128)S(1)}, f32[112,128]{1,0:T(8,128)S(1)}, u32[]{:S(2)}, u32[]{:S(2)}) collective-permute-start(f32[112,128]{1,0:T(8,128)S(1)} %add_add_fusion), channel_id=1, source_target_pairs={{0,1},{1,0},{2,3},{3,2},{4,5},{5,4},{6,7},{7,6},{8,9},{9,8},{10,11... | collective-permute-start | bytes 172040 | tf_op jit(solution)/shard_map/mean1/ppermute | solution.py:211
  33.8 6.4 %copy-start = (f32[16,28672]{1,0:T(8,128)S(1)}, f32[16,28672]{1,0:T(8,128)}, u32[]{:S(2)}) copy-start(f32[16,28672]{1,0:T(8,128)} %base.9) | copy-start | bytes 5505028
  33.8 6.4 %copy-start.1 = (f32[16,28672]{1,0:T(8,128)S(1)}, f32[16,28672]{1,0:T(8,128)}, u32[]{:S(2)}) copy-start(f32[16,28672]{1,0:T(8,128)} %mom.3) | copy-start | bytes 5505028
  37.4 4.6 %collective-permute-start.15 = (f32[4,112,128]{2,1,0:T(8,128)S(1)}, f32[4,112,128]{2,1,0:T(8,128)S(1)}, u32[]{:S(2)}, u32[]{:S(2)}) collective-permute-start(f32[4,112,128]{2,1,0:T(8,128)S(1)} %pad_maximum_fusion.refs_0_), channel_id=1, source_target_pairs={{0,16},{16,0},{32,48},{48,32},{64,80},{80,64},{96,112},{112,96},{1... | collective-permute-start | bytes 688136 | tf_op jit(solution)/shard_map/swap1/ppermute | solution.py:215
